TPU v7x, 512 devices: a whole 4x8x8 slice. The times are simulated.
512 devices in a mesh: ep: 64 (over z, x, core), dp: 8 (over y).
Axes of the slice: x: 4, y: 8, z: 8, core: 2. Of those that a mesh axis runs over, the one named last changes fastest.
Arguments:
- tokens: bfloat16 [4096, 4096], P('ep', 'dp'), may hold values from -6 to 6
- expert_ids: int32 [4096, 8], P('ep'), may hold values from 0 to 63, all different within a row
- gate_logits: float32 [4096, 8], P('ep'), may hold values from -6 to 6
- placement: int32 [32], replicated, may hold values from 0 to 63, as said below
- split_rows: int32 [32], replicated, may hold values from 0 to 8
- gate_up_weight: bfloat16 [64, 4096, 2, 1024], P('ep', None, None, 'dp'), may hold values from -0.09375 to 0.09375
- down_weight: bfloat16 [64, 1024, 4096], P('ep', None, 'dp'), may hold values from -0.1875 to 0.1875
- spare_gate_up: bfloat16 [64, 4096, 2, 512], P('ep', None, None, 'dp'), may hold values from -0.09375 to 0.09375
- spare_down: bfloat16 [64, 512, 4096], P('ep', None, 'dp'), may hold values from -0.1875 to 0.1875
Outputs:
- mixed: bfloat16 [4096, 4096], P('ep', 'dp')
Inputs may be any that keep to these rules, and one draw needn't show every extreme that they name: `expert_ids`: each token names 8 different experts. `placement`: 32 different experts.
All inputs are finite; a program needn't handle non-finite values.
Results may differ from a plain program's by a relative error of at most 0.0058.
Values may be sent and summed in bfloat16 or wider, within the bound.
A program may use at most 64 MiB of HBM per device.

v0:
```python
import jax
import jax.numpy as jnp
from jax import lax
from jax.sharding import PartitionSpec as P


def rank_pairs(chosen_ids, experts):
    per_group = chosen_ids.shape[0]
    which = (chosen_ids[:, None] == jnp.arange(experts, dtype=jnp.int32)[None, :]).astype(
        jnp.float32
    )
    ordinal = jnp.arange(per_group, dtype=jnp.int32)
    earlier = (ordinal[None, :] < ordinal[:, None]).astype(jnp.float32)
    before = jnp.dot(
        earlier, which, preferred_element_type=jnp.float32, precision=lax.Precision.HIGHEST
    )
    return jnp.sum(before * which, axis=1).astype(jnp.int32)


def gate_up(row_block, weight):
    gate_both = jnp.einsum("...d,djf->...jf", row_block, weight, preferred_element_type=jnp.float32)
    return (jax.nn.silu(gate_both[..., 0, :]) * gate_both[..., 1, :]).astype(jnp.bfloat16)


def per_device(
    tokens,
    expert_ids,
    gate_logits,
    placement,
    split_rows,
    gate_up_weight,
    down_weight,
    spare_gate_up,
    spare_down,
):
    ep_count = lax.axis_size("ep")
    dp_count = lax.axis_size("dp")
    whole_rows = lax.all_gather(tokens, "dp", axis=1, tiled=True)
    group_tokens, d_model = whole_rows.shape
    top_count = expert_ids.shape[1]
    spares = placement.shape[0]
    capacity = group_tokens * top_count // ep_count
    per_group = group_tokens * top_count
    chosen_ids = expert_ids.reshape(per_group)
    pair_rank = rank_pairs(chosen_ids, ep_count)
    is_match = chosen_ids[:, None] == placement[None, :]
    is_hot = jnp.any(is_match, axis=1)
    copy_index = jnp.sum(
        jnp.where(is_match, jnp.arange(spares, dtype=jnp.int32)[None, :], 0), axis=1
    )
    split_here = jnp.sum(jnp.where(is_match, split_rows[None, :], 0), axis=1)
    to_copy = is_hot & (pair_rank >= split_here)
    slot_of = jnp.where(to_copy, ep_count + copy_index, chosen_ids)
    position = jnp.where(to_copy, pair_rank - split_here, pair_rank)
    kept_mask = position < capacity
    flat_slot = slot_of * capacity + position
    slot_total = (ep_count + spares) * capacity
    row_table = jnp.full((slot_total,), group_tokens, jnp.int32)
    row_table = row_table.at[jnp.where(kept_mask, flat_slot, slot_total)].set(
        jnp.arange(per_group, dtype=jnp.int32) // top_count, mode="drop"
    )
    padded = jnp.concatenate([whole_rows, jnp.zeros((1, d_model), whole_rows.dtype)], axis=0)
    send_all = jnp.take(padded, row_table, axis=0)
    home_send = send_all[: ep_count * capacity].reshape(ep_count, capacity, d_model)
    spare_table = send_all[ep_count * capacity :].reshape(spares, capacity, d_model)
    own_gu = gate_up_weight[0]
    own_dn = down_weight[0]
    extra_gu = spare_gate_up[0]
    extra_dn = spare_down[0]
    home_rows, spare_rows = (
        lax.all_to_all(home_send, "ep", split_axis=0, concat_axis=0, tiled=True),
        lax.all_to_all(
            jnp.repeat(spare_table, 2, axis=0), "ep", split_axis=0, concat_axis=0, tiled=True
        ),
    )
    home_hidden = gate_up(home_rows, own_gu)
    spare_hidden = gate_up(spare_rows, extra_gu)
    unit_piece = spare_hidden.shape[2]
    stacked = jnp.concatenate(
        [home_hidden.reshape(ep_count, capacity, 2, unit_piece), spare_hidden[:, :, None, :]],
        axis=2,
    )
    columns = own_dn.shape[1]
    home_view = jnp.transpose(
        own_dn.reshape(dp_count, 2, unit_piece, columns), (1, 0, 2, 3)
    ).reshape(2, dp_count * unit_piece, columns)
    piece = lax.all_gather(stacked, "dp", axis=3, tiled=True)
    home_term = jnp.einsum(
        "gchf,hfe->gce", piece[:, :, 0:2], home_view, preferred_element_type=jnp.float32
    )
    spare_term = jnp.einsum(
        "gcf,fe->gce", piece[:, :, 2], extra_dn, preferred_element_type=jnp.float32
    )
    home_out = home_term.astype(jnp.bfloat16)
    home_back = lax.all_to_all(home_out, "ep", split_axis=0, concat_axis=0, tiled=True)
    halves_back = lax.all_to_all(spare_term, "ep", split_axis=0, concat_axis=0, tiled=True)
    spare_back = jnp.sum(halves_back.reshape(spares, 2, capacity, columns), axis=1).astype(
        jnp.bfloat16
    )
    table = jnp.concatenate(
        [
            home_back.reshape(ep_count * capacity, columns),
            spare_back.reshape(spares * capacity, columns),
        ],
        axis=0,
    )
    chosen = jnp.take(table, jnp.where(kept_mask, flat_slot, 0), axis=0).reshape(
        group_tokens, top_count, columns
    )
    gate_score = jax.nn.sigmoid(gate_logits)
    gate_weight = 2.5 * gate_score / jnp.sum(gate_score, axis=1, keepdims=True)
    kept_weight = jnp.where(kept_mask.reshape(group_tokens, top_count), gate_weight, 0.0)
    mixed = jnp.sum(kept_weight[:, :, None] * chosen.astype(jnp.float32), axis=1)
    return mixed.astype(jnp.bfloat16)


def solution(mesh):
    return jax.shard_map(
        per_device,
        mesh=mesh,
        in_specs=(
            P("ep", "dp"),
            P("ep", None),
            P("ep", None),
            P(),
            P(),
            P("ep", None, None, "dp"),
            P("ep", None, "dp"),
            P("ep", None, None, "dp"),
            P("ep", None, "dp"),
        ),
        out_specs=P("ep", "dp"),
        check_vma=False,
    )
```

profile of v0, /device:TPU:1, one launch (start us, length us, event | category | flops | bytes accessed | tf_op | source)
XLA Modules:
  0.0 393.3 jit_solution(9340579253816340319)
XLA Ops:
  9.5 2.4 scatter_custom_fusion
  12.0 21.9 %all_gather.6 = bf16[64,4096]{1,0:T(8,128)(2,1)S(1)} all-gather(bf16[64,512]{1,0:T(8,128)(2,1)} %param.9), channel_id=1, replica_groups=mesh['ep'=64,'dp'=8] {'dp'}, dimensions={1}, use_global_device_ids=true | all-gather | bytes 589824 | tf_op jit(solution)/shard_map/all_gather | solution.py:38
  33.9 5.7 %gather_fusion = bf16[768,4096]{1,0:T(8,128)(2,1)} fusion(bf16[65,4096]{1,0:T(8,128)(2,1)S(1)} %concatenate.9, s32[1024]{0:T(1024)S(1)} %pad_clamp_fusion.1), kind=kCustom, calls=%fused_computation | custom fusion | bytes 12585984 | tf_op jit(solution)/shard_map/jit(_take)/gather | solution.py:63
  39.7 3.4 broadcast_select_fusion
  43.1 2.7 copy-done.1
  45.7 2.3 slice_bitcast_fusion
  48.1 20.2 %all-to-all-start = ((bf16[64,8,4096]{2,1,0:T(8,128)(2,1)}), bf16[64,8,4096]{2,1,0:T(8,128)(2,1)}, u32[]{:S(2)}, u32[]{:S(2)}) async-start(bf16[64,8,4096]{2,1,0:T(8,128)(2,1)} %slice_bitcast_fusion), calls=%async_computation | async-start | bytes 8388608 | tf_op jit(solution)/shard_map/all_to_all | solution.py:71
  68.3 1.7 slice_bitcast_fusion.1
  70.1 92.7 %all-to-all-done = bf16[64,8,4096]{2,1,0:T(8,128)(2,1)} async-done(((bf16[64,8,4096]{2,1,0:T(8,128)(2,1)}), bf16[64,8,4096]{2,1,0:T(8,128)(2,1)}, u32[]{:S(2)}, u32[]{:S(2)}) %all-to-all-start) | async-done | bytes 4194336 | tf_op jit(solution)/shard_map/all_to_all | solution.py:71
  162.7 2.6 broadcast_in_dim.82
  165.3 7.4 %all-to-all-start.1 = ((bf16[64,8,4096]{2,1,0:T(8,128)(2,1)}), bf16[64,8,4096]{2,1,0:T(8,128)(2,1)}, u32[]{:S(2)}, u32[]{:S(2)}) async-start(bf16[64,8,4096]{2,1,0:T(8,128)(2,1)} %bitcast.67), calls=%async_computation.1 | async-start | bytes 8388608 | tf_op jit(solution)/shard_map/all_to_all | solution.py:72
  172.9 4.1 %fusion.2 = f32[64,8,2,128]{3,1,2,0:T(8,128)S(1)} fusion(bf16[64,8,4096]{2,1,0:T(8,128)(2,1)} %all-to-all-done, bf16[4096,2,128]{2,1,0:T(2,128)(2,1)} %bitcast.79), kind=kOutput, calls=%fused_computation.7 | convolution fusion | flops 1073741824 | bytes 6815744 | tf_op jit(solution)/shard_map/...d,djf->...jf/dot_general | solution.py:21
  178.6 88.7 %all-to-all-done.1 = bf16[64,8,4096]{2,1,0:T(8,128)(2,1)} async-done(((bf16[64,8,4096]{2,1,0:T(8,128)(2,1)}), bf16[64,8,4096]{2,1,0:T(8,128)(2,1)}, u32[]{:S(2)}, u32[]{:S(2)}) %all-to-all-start.1) | async-done | bytes 4194336 | tf_op jit(solution)/shard_map/all_to_all | solution.py:72
  267.4 3.5 fusion
  272.1 43.2 %all-gather.2.cloned.1.call-done = bf16[64,8,3,512]{0,1,2,3:T(8,128)(2,1)} async-done(((bf16[64,8,3,64]{0,1,2,3:T(8,128)(2,1)}), bf16[64,8,3,512]{0,1,2,3:T(8,128)(2,1)}) %all-gather.2.cloned.1.call-update) | async-done | bytes 1572880 | tf_op jit(solution)/shard_map/all_gather | solution.py:87
  317.9 1.4 fusion.9
  319.3 11.9 %all-to-all-start.3 = ((f32[64,8,512]{2,1,0:T(8,128)}), f32[64,8,512]{2,1,0:T(8,128)}, u32[]{:S(2)}, u32[]{:S(2)}) async-start(f32[64,8,512]{2,1,0:T(8,128)} %fusion.9), calls=%async_computation.3 | async-start | bytes 2097152 | tf_op jit(solution)/shard_map/all_to_all | solution.py:96
  331.3 2.3 copy.48
  333.6 3.6 copy.53
  337.2 3.1 fusion.6
  340.3 18.9 %all-to-all-done.3 = f32[64,8,512]{2,1,0:T(8,128)} async-done(((f32[64,8,512]{2,1,0:T(8,128)}), f32[64,8,512]{2,1,0:T(8,128)}, u32[]{:S(2)}, u32[]{:S(2)}) %all-to-all-start.3) | async-done | bytes 1048608 | tf_op jit(solution)/shard_map/all_to_all | solution.py:96
  359.2 6.5 %all-to-all-start.2 = ((bf16[64,8,512]{2,1,0:T(8,128)(2,1)}), bf16[64,8,512]{2,1,0:T(8,128)(2,1)S(1)}, u32[]{:S(2)}, u32[]{:S(2)}) async-start(bf16[64,8,512]{2,1,0:T(8,128)(2,1)} %fusion.6), calls=%async_computation.2 | async-start | bytes 1048576 | tf_op jit(solution)/shard_map/all_to_all | solution.py:95
  367.7 15.6 %all-to-all-done.2 = bf16[64,8,512]{2,1,0:T(8,128)(2,1)S(1)} async-done(((bf16[64,8,512]{2,1,0:T(8,128)(2,1)}), bf16[64,8,512]{2,1,0:T(8,128)(2,1)S(1)}, u32[]{:S(2)}, u32[]{:S(2)}) %all-to-all-start.2) | async-done | bytes 524320 | tf_op jit(solution)/shard_map/all_to_all | solution.py:95
  383.4 2.0 gather_fusion.1
  (49 shorter events, 11.6 us)
Async XLA Ops:
  6.5 260.8 %copy-start = (bf16[1,4096,2,64]{1,3,2,0:T(8,128)(2,1)S(1)}, bf16[1,4096,2,64]{1,3,2,0:T(8,128)(2,1)}, u32[]{:S(2)}) copy-start(bf16[1,4096,2,64]{1,3,2,0:T(8,128)(2,1)} %param.16) | copy-start | bytes 3145732
  43.1 2.7 copy-start.1
  48.1 114.6 %all-to-all-start = ((bf16[64,8,4096]{2,1,0:T(8,128)(2,1)}), bf16[64,8,4096]{2,1,0:T(8,128)(2,1)}, u32[]{:S(2)}, u32[]{:S(2)}) async-start(bf16[64,8,4096]{2,1,0:T(8,128)(2,1)} %slice_bitcast_fusion), calls=%async_computation | async-start | bytes 8388608 | tf_op jit(solution)/shard_map/all_to_all | solution.py:71
  165.3 102.0 %all-to-all-start.1 = ((bf16[64,8,4096]{2,1,0:T(8,128)(2,1)}), bf16[64,8,4096]{2,1,0:T(8,128)(2,1)}, u32[]{:S(2)}, u32[]{:S(2)}) async-start(bf16[64,8,4096]{2,1,0:T(8,128)(2,1)} %bitcast.67), calls=%async_computation.1 | async-start | bytes 8388608 | tf_op jit(solution)/shard_map/all_to_all | solution.py:72
  172.7 142.7 %all-gather.2.cloned.1.call-start = ((), (), s32[]{:S(2)}) async-start(), calls=%async_computation.4 | async-start | bytes 3538944 | tf_op jit(solution)/shard_map/all_gather | solution.py:87
  270.8 47.1 %copy-start.2 = (bf16[1,512,512]{2,1,0:T(8,128)(2,1)S(1)}, bf16[1,512,512]{2,1,0:T(8,128)(2,1)}, u32[]{:S(2)}) copy-start(bf16[1,512,512]{2,1,0:T(8,128)(2,1)} %param.17) | copy-start | bytes 1572868
  319.3 14.3 %slice-start = ((bf16[64,8,3,512]{0,1,2,3:T(8,128)(2,1)}), bf16[64,8,2,512]{0,1,2,3:T(8,128)(2,1)S(1)}, s32[]{:S(2)}) async-start(bf16[64,8,3,512]{0,1,2,3:T(8,128)(2,1)} %all-gather.2.cloned.1.call-done), calls=%async_computation.5 | async-start | bytes 4194304 | tf_op jit(solution)/shard_map/slice | solution.py:89
  319.3 39.8 %all-to-all-start.3 = ((f32[64,8,512]{2,1,0:T(8,128)}), f32[64,8,512]{2,1,0:T(8,128)}, u32[]{:S(2)}, u32[]{:S(2)}) async-start(f32[64,8,512]{2,1,0:T(8,128)} %fusion.9), calls=%async_computation.3 | async-start | bytes 2097152 | tf_op jit(solution)/shard_map/all_to_all | solution.py:96
  333.6 32.4 %copy-start.3 = (f32[64,8]{0,1:T(8,128)S(1)}, f32[64,8]{0,1:T(8,128)}, u32[]{:S(2)}) copy-start(f32[64,8]{0,1:T(8,128)} %param.11) | copy-start | bytes 6148
  359.2 24.2 %all-to-all-start.2 = ((bf16[64,8,512]{2,1,0:T(8,128)(2,1)}), bf16[64,8,512]{2,1,0:T(8,128)(2,1)S(1)}, u32[]{:S(2)}, u32[]{:S(2)}) async-start(bf16[64,8,512]{2,1,0:T(8,128)(2,1)} %fusion.6), calls=%async_computation.2 | async-start | bytes 1048576 | tf_op jit(solution)/shard_map/all_to_all | solution.py:95
Sparse Core Ops, SparseCore 0:
  272.2 43.0 all-gather.1
where the time goes:
time: 394 us; the launch traced here: 393 us
  waiting for transfers between devices  259 us (66%)
  starting transfers between devices  46.2 us (12%)
  local copies, waits for them, and re-layouts  31.1 us (8%)
  blocking collectives  21.9 us (6%)
  between operations  13.7 us (3%)
  matrix products  12.3 us (3%)
  other arithmetic  8.74 us (2%)
    all_to_all x1, waiting for transfers between devices, per_device(): lax.all_to_all(home_send, 'ep', split_axis=0, concat_axis=0, tiled=True)  92.7 us
    all_to_all x1, waiting for transfers between devices, per_device(): lax.all_to_all(jnp.repeat(spare_table, 2, axis=0), 'ep', split_axis=0, co...  88.7 us
    all_gather x1, waiting for transfers between devices, per_device(): piece = lax.all_gather(stacked, 'dp', axis=3, tiled=True)  43.2 us
    all_gather x1, blocking collectives, per_device(): whole_rows = lax.all_gather(tokens, 'dp', axis=1, tiled=True)  21.9 us
    all_to_all x1, starting transfers between devices, per_device(): lax.all_to_all(home_send, 'ep', split_axis=0, concat_axis=0, tiled=True)  20.2 us
    all_to_all x1, waiting for transfers between devices, per_device(): lax.all_to_all(spare_term, 'ep', split_axis=0, concat_axis=0, tiled=True)  18.9 us
    all_to_all x1, waiting for transfers between devices, per_device(): lax.all_to_all(home_out, 'ep', split_axis=0, concat_axis=0, tiled=True)  15.6 us
    all_to_all x1, starting transfers between devices, per_device(): lax.all_to_all(spare_term, 'ep', split_axis=0, concat_axis=0, tiled=True)  11.9 us
  transfers between devices with their start and end apart: 5, of which 5 were waited for; matrix products, arithmetic and copies ran while one was open for 5% of the time, Pallas kernels for 0%

commit v1 on v0

v1 whole, which is shorter than its diff:
```python
import functools

import jax
import jax.numpy as jnp
from jax import lax
from jax.experimental import pallas as pl
from jax.experimental.pallas import tpu as pltpu
from jax.sharding import PartitionSpec as P

MESH = pl.DeviceIdType.MESH
F32 = jnp.float32
BF16 = jnp.bfloat16
CHUNKS = 4
CW, CCW = 0, 1


def hops(chunk, way):
    return 4 if chunk % 2 == way else 3


def expert_kernel(
    rows_ref, wh_ref, ws_ref, dh_ref, ds_ref, out_ref,
    feat, pair_feat, hid, acc_h, acc_s, dspare, part, pair_part,
    ring_send, ring_recv, pair_send, pair_recv, hid_send, hid_recv, part_send, part_recv,
):
    n_dp = 8
    ep = lax.axis_index("ep")
    me = lax.axis_index("dp")
    core = lax.rem(ep, 2)
    sibling = {"ep": ep + 1 - 2 * core, "dp": me}
    ring = (
        {"ep": ep, "dp": lax.rem(me + 1, n_dp)},
        {"ep": ep, "dp": lax.rem(me + n_dp - 1, n_dp)},
    )
    total = rows_ref.shape[0]
    rows = total // CHUNKS
    width = wh_ref.shape[0] // n_dp
    half = width // 2
    units = wh_ref.shape[1] // 2

    barrier = pltpu.get_barrier_semaphore()
    for other in (ring[0], ring[1], sibling):
        pl.semaphore_signal(barrier, inc=1, device_id=other, device_id_type=MESH)
    pl.semaphore_wait(barrier, 3)

    def source(way, hop):
        return lax.rem(me + (n_dp - hop if way == CW else hop), n_dp)

    def feat_copy(chunk, way, hop):
        src = source(way, hop - 1)
        window = pl.ds(chunk * rows, rows)
        return pltpu.make_async_remote_copy(
            src_ref=rows_ref.at[window] if hop == 1 else feat.at[src, window],
            dst_ref=feat.at[src, window],
            send_sem=ring_send.at[chunk, way, hop - 1],
            recv_sem=ring_recv.at[chunk, way, hop - 1],
            device_id=ring[way], device_id_type=MESH,
        )

    def pair_copy(chunk, way, hop):
        src = source(way, hop)
        window = pl.ds(chunk * rows, rows)
        block = rows_ref.at[window, pl.ds(width, half)] if hop == 0 else feat.at[src, window, pl.ds(width, half)]
        return pltpu.make_async_remote_copy(
            src_ref=block,
            dst_ref=pair_feat.at[src, window],
            send_sem=pair_send.at[chunk, way, hop],
            recv_sem=pair_recv.at[chunk, way, hop],
            device_id=sibling, device_id_type=MESH,
        )

    hid_rows = rows + rows // 2

    def hid_copy(chunk, way, hop):
        src = source(way, hop - 1)
        window = pl.ds(chunk * hid_rows, hid_rows)
        return pltpu.make_async_remote_copy(
            src_ref=hid.at[src, window],
            dst_ref=hid.at[src, window],
            send_sem=hid_send.at[chunk, way, hop - 1],
            recv_sem=hid_recv.at[chunk, way, hop - 1],
            device_id=ring[way], device_id_type=MESH,
        )

    out_half = ds_ref.shape[1] // 2

    def part_copy(chunk):
        window = pl.ds(chunk * rows, rows)
        return pltpu.make_async_remote_copy(
            src_ref=part.at[window, pl.ds((1 - core) * out_half, out_half)],
            dst_ref=pair_part.at[window],
            send_sem=part_send.at[chunk],
            recv_sem=part_recv.at[chunk],
            device_id=sibling, device_id_type=MESH,
        )

    def begin(chunk):
        for way in (CW, CCW):
            feat_copy(chunk, way, 1).start()
        pair_copy(chunk, CW, 0).start()

    def first_half(chunk):
        window = pl.ds(chunk * rows, rows)
        for way in (CW, CCW):
            for hop in range(0 if way == CW else 1, hops(chunk, way) + 1):
                pair_copy(chunk, way, hop).wait_recv()

        def term(block, other, at):
            x = block[:, :width]
            w = wh_ref[pl.ds(pl.multiple_of(at * width, width), width), :]
            home = jnp.dot(x, w, preferred_element_type=F32)
            own_at = pl.ds(pl.multiple_of(at * width + core * half, half), half)
            other_at = pl.ds(pl.multiple_of(at * width + (1 - core) * half, half), half)
            dims = (((1,), (1,)), ((), ()))
            spare = lax.dot_general(block[:, width:], ws_ref[:, own_at], dims, preferred_element_type=F32)
            spare += lax.dot_general(other, ws_ref[:, other_at], dims, preferred_element_type=F32)
            return home, spare

        acc_h[...], acc_s[...] = term(rows_ref[window, :], pair_feat[me, window, :], me)

        @pl.loop(1, n_dp)
        def _(step):
            at = lax.rem(me + step, n_dp)
            home, spare = term(feat[at, window, :], pair_feat[at, window, :], at)
            acc_h[...] += home
            acc_s[...] += spare

        gate = acc_h[:, :units]
        base = chunk * hid_rows
        hid[me, pl.ds(base, rows), :] = (gate / (1.0 + jnp.exp(-gate)) * acc_h[:, units:]).astype(BF16)
        plain = acc_s[...]
        turned = pltpu.roll(plain, units // 2, 1)
        low = lax.broadcasted_iota(jnp.int32, plain.shape, 1) < units // 2
        gate = jnp.where(low, plain, turned)
        both = gate / (1.0 + jnp.exp(-gate)) * jnp.where(low, turned, plain)
        top = rows // 2
        packed = jnp.where(low[:top], both[:top], both[top:])
        hid[me, pl.ds(base + rows, top), :] = packed.astype(BF16)
        for way in (CW, CCW):
            hid_copy(chunk, way, 1).start()

    def second_half(chunk):
        window = pl.ds(chunk * rows, rows)
        base = chunk * hid_rows
        top = rows // 2
        both = jnp.concatenate([hid[at, pl.ds(base + rows, top), :] for at in range(n_dp)], axis=1)
        term = jnp.dot(both, dspare[...], preferred_element_type=F32)
        columns = ds_ref.shape[1]
        part[pl.ds(chunk * rows, top), :] = term[:, :columns]
        part[pl.ds(chunk * rows + top, top), :] = term[:, columns:]
        part_copy(chunk).start()
        whole = jnp.concatenate([hid[at, pl.ds(base, rows), :] for at in range(n_dp)], axis=1)
        out_ref[window, pl.ds(0, columns)] = jnp.dot(whole, dh_ref[...], preferred_element_type=F32).astype(BF16)

    def finish(chunk):
        window = pl.ds(chunk * rows, rows)
        part_copy(chunk).wait_recv()
        own = part[window, pl.ds(pl.multiple_of(core * out_half, out_half), out_half)]
        out_ref[window, pl.ds(2 * out_half, out_half)] = (own + pair_part[window, :]).astype(BF16)

    begin(0)
    begin(1)
    zero = jnp.zeros((units // 2, ds_ref.shape[1]), BF16)
    for at in range(n_dp):
        w = ds_ref[pl.ds(at * units // 2, units // 2), :]
        dspare[pl.ds(at * units, units // 2), :] = jnp.concatenate([w, zero], axis=1)
        dspare[pl.ds(at * units + units // 2, units // 2), :] = jnp.concatenate([zero, w], axis=1)

    def arrive(chunk, hop):
        for way in (CW, CCW):
            if hop <= hops(chunk, way):
                feat_copy(chunk, way, hop).wait_recv()
                if hop < hops(chunk, way):
                    feat_copy(chunk, way, hop + 1).start()
                pair_copy(chunk, way, hop).start()

    def hid_arrive(chunk, hop):
        for way in (CW, CCW):
            if hop <= hops(chunk, way):
                hid_copy(chunk, way, hop).wait_recv()
                if hop < hops(chunk, way):
                    hid_copy(chunk, way, hop + 1).start()

    for first in range(0, CHUNKS, 2):
        for hop in range(1, 5):
            for chunk in (first, first + 1):
                arrive(chunk, hop)
                if hop >= 3 and chunk + 2 < CHUNKS and hop == 3:
                    begin(chunk + 2)
                if first >= 2:
                    hid_arrive(chunk - 2, hop)
        for chunk in (first, first + 1):
            if first >= 2:
                second_half(chunk - 2)
            first_half(chunk)
    for hop in range(1, 5):
        for chunk in (CHUNKS - 2, CHUNKS - 1):
            hid_arrive(chunk, hop)
    for chunk in (CHUNKS - 2, CHUNKS - 1):
        second_half(chunk)
    for chunk in range(CHUNKS):
        finish(chunk)
    for chunk in range(CHUNKS):
        for way in (CW, CCW):
            for hop in range(1, hops(chunk, way) + 1):
                feat_copy(chunk, way, hop).wait_send()
                hid_copy(chunk, way, hop).wait_send()
                pair_copy(chunk, way, hop).wait_send()
        pair_copy(chunk, CW, 0).wait_send()
        part_copy(chunk).wait_send()


def experts(rows, wh, ws, dh, ds):
    total, width3 = rows.shape
    n_dp = 8
    width = wh.shape[0] // n_dp
    units = wh.shape[1] // 2
    chunk_rows = total // CHUNKS
    ring_sems = pltpu.SemaphoreType.DMA((CHUNKS, 2, 4))
    pair_sems = pltpu.SemaphoreType.DMA((CHUNKS, 2, 5))
    part_sems = pltpu.SemaphoreType.DMA((CHUNKS,))
    return pl.pallas_call(
        expert_kernel,
        out_shape=jax.ShapeDtypeStruct((total, width3), BF16),
        in_specs=[pl.BlockSpec(memory_space=pltpu.VMEM)] * 5,
        out_specs=pl.BlockSpec(memory_space=pltpu.VMEM),
        scratch_shapes=[
            pltpu.VMEM((n_dp, total, width3), BF16),
            pltpu.VMEM((n_dp, total, width // 2), BF16),
            pltpu.VMEM((n_dp, total + total // 2, units), BF16),
            pltpu.VMEM((chunk_rows, 2 * units), F32),
            pltpu.VMEM((chunk_rows, units), F32),
            pltpu.VMEM((n_dp * units, 2 * width), BF16),
            pltpu.VMEM((total, ds.shape[1]), F32),
            pltpu.VMEM((total, ds.shape[1] // 2), F32),
            ring_sems, ring_sems, pair_sems, pair_sems, ring_sems, ring_sems, part_sems, part_sems,
        ],
        compiler_params=pltpu.CompilerParams(
            collective_id=0, has_side_effects=True, vmem_limit_bytes=56 * 1024 * 1024
        ),
    )(rows, wh, ws, dh, ds)


def route(expert_ids, placement, split_rows, slots, capacity):
    per_group = expert_ids.shape[0] * expert_ids.shape[1]
    chosen = expert_ids.reshape(per_group)
    ordinal = jnp.arange(per_group, dtype=jnp.int32)
    same = (chosen[:, None] == chosen[None, :]) & (ordinal[None, :] < ordinal[:, None])
    rank = jnp.sum(same.astype(jnp.int32), axis=1)
    match = chosen[:, None] == placement[None, :]
    hot = jnp.any(match, axis=1)
    copy = jnp.sum(jnp.where(match, jnp.arange(placement.shape[0], dtype=jnp.int32)[None, :], 0), axis=1)
    split = jnp.sum(jnp.where(match, split_rows[None, :], 0), axis=1)
    moved = hot & (rank >= split)
    slot = jnp.where(moved, slots + copy, chosen)
    position = jnp.where(moved, rank - split, rank)
    return jnp.where(position < capacity, slot * capacity + position, -1).reshape(expert_ids.shape)


def per_device(
    tokens, expert_ids, gate_logits, placement, split_rows,
    gate_up_weight, down_weight, spare_gate_up, spare_down,
):
    n_ep = lax.axis_size("ep")
    spares = placement.shape[0]
    capacity = 8
    width = tokens.shape[1]
    half = width // 2
    table_row = route(expert_ids, placement, split_rows, n_ep, capacity)
    slot_rows = (n_ep + spares) * capacity
    hit = table_row[None] == jnp.arange(slot_rows, dtype=jnp.int32)[:, None, None]
    pick = jnp.any(hit, axis=2).astype(BF16)
    sent = jnp.dot(pick, tokens, preferred_element_type=F32).astype(BF16)
    home = sent[: n_ep * capacity].reshape(n_ep, capacity, width)
    extra = sent[n_ep * capacity :].reshape(spares, capacity, 2, half)
    extra = jnp.transpose(extra, (0, 2, 1, 3)).reshape(n_ep, capacity, half)
    send = jnp.concatenate([home, extra], axis=2)
    rows = lax.all_to_all(send, "ep", split_axis=0, concat_axis=0, tiled=True)
    wh = gate_up_weight[0].reshape(gate_up_weight.shape[1], -1)
    ws = jnp.transpose(spare_gate_up[0], (1, 2, 0)).reshape(-1, spare_gate_up.shape[1])
    out = experts(rows.reshape(n_ep * capacity, width + half), wh, ws, down_weight[0], spare_down[0])
    back = lax.all_to_all(
        out.reshape(n_ep, capacity, width + half), "ep", split_axis=0, concat_axis=0, tiled=True
    ).reshape(n_ep * capacity, width + half)
    score = jax.nn.sigmoid(gate_logits)
    weight = 2.5 * score / jnp.sum(score, axis=1, keepdims=True)
    matrix = jnp.sum(jnp.where(hit, weight[None], 0.0), axis=2).T
    home_matrix = matrix[:, : n_ep * capacity]
    extra_matrix = matrix[:, n_ep * capacity :].reshape(-1, spares, 1, capacity)
    side = jnp.arange(2)[None, :, None, None, None] == jnp.arange(2)[None, None, None, :, None]
    extra_matrix = jnp.where(side, extra_matrix[:, None], 0.0).reshape(-1, n_ep * capacity)

    def exact_dot(a, b):
        high = lax.reduce_precision(a, 8, 7)
        low = (a - high).astype(BF16)
        return jnp.dot(high.astype(BF16), b, preferred_element_type=F32) + jnp.dot(low, b, preferred_element_type=F32)

    mixed = exact_dot(home_matrix, back[:, :width])
    extra = exact_dot(extra_matrix, back[:, width:]).reshape(-1, 2 * half)
    return (mixed + extra).astype(BF16)


def solution(mesh):
    return jax.shard_map(
        per_device,
        mesh=mesh,
        in_specs=(
            P("ep", "dp"),
            P("ep", None),
            P("ep", None),
            P(),
            P(),
            P("ep", None, None, "dp"),
            P("ep", None, "dp"),
            P("ep", None, None, "dp"),
            P("ep", None, "dp"),
        ),
        out_specs=P("ep", "dp"),
        check_vma=False,
    )
```

time: 394 us -> 176 us (0.45)
  waiting for transfers between devices: 259 us -> 29.9 us
  Pallas kernels: 0 us -> 102 us
  starting transfers between devices: 46.2 us -> 20.5 us
  blocking collectives: 21.9 us -> 0 us
  local copies, waits for them, and re-layouts: 31.1 us -> 12.9 us
  between operations: 13.7 us -> 0.22 us
  matrix products: 12.3 us -> 1.84 us
    all_to_all x4 -> x2, waiting for transfers between devices: 216 us -> 29.9 us  [the longest x1 21.1 us: per_device(): rows = lax.all_to_all(send, 'ep', split_axis=0, concat_axis=0, tiled=True)]
    pallas_call x0 -> x1, Pallas kernels: none -> 102 us  [experts(): pl.pallas_call(expert_kernel, out_shape=jax.ShapeDtypeStruct((total, widt...]
    all_gather x1 -> x0, waiting for transfers between devices: 43.2 us -> none  [per_device(): piece = lax.all_gather(stacked, 'dp', axis=3, tiled=True)]
    all_to_all x4 -> x2, starting transfers between devices: 46 us -> 20.5 us  [the longest x1 14.8 us: per_device(): rows = lax.all_to_all(send, 'ep', split_axis=0, concat_axis=0, tiled=True)]
    all_gather x1 -> x0, blocking collectives: 21.9 us -> none  [per_device(): whole_rows = lax.all_gather(tokens, 'dp', axis=1, tiled=True)]
    dot_general x5, matrix products: 12.3 us -> 1.84 us  [the longest x2 1.03 us: exact_dot(): jnp.dot(low, b, preferred_element_type=F32)]
    select_n x0 -> x1, local copies, waits for them, and re-layouts: none -> 7.89 us  [per_device(): jnp.where(side, extra_matrix[:, None], 0.0).reshape(-1, n_ep * capacity)]
    gather x2 -> x0, local copies, waits for them, and re-layouts: 7.7 us -> none  [the longest x1 5.72 us: per_device(): send_all = jnp.take(padded, row_table, axis=0)]
  transfers between devices with their start and end apart: 5 -> 2, of which waited for: 5 -> 2; matrix products, arithmetic and copies ran while one was open for 5% -> 9% of each run, Pallas kernels for 0% -> 0%
where the time goes in v1:
time: 176 us; the launch traced here: 175 us
  Pallas kernels  102 us (58%)
  waiting for transfers between devices  29.9 us (17%)
  starting transfers between devices  20.5 us (12%)
  local copies, waits for them, and re-layouts  12.9 us (7%)
  other arithmetic  8.18 us (5%)
  matrix products  1.84 us (1%)
    pallas_call x1, Pallas kernels, experts(): pl.pallas_call(expert_kernel, out_shape=jax.ShapeDtypeStruct((total, widt...  102 us
    all_to_all x1, waiting for transfers between devices, per_device(): rows = lax.all_to_all(send, 'ep', split_axis=0, concat_axis=0, tiled=True)  21.1 us
    all_to_all x1, starting transfers between devices, per_device(): rows = lax.all_to_all(send, 'ep', split_axis=0, concat_axis=0, tiled=True)  14.8 us
    all_to_all x1, waiting for transfers between devices, per_device(): lax.all_to_all(out.reshape(n_ep, capacity, width + half), 'ep', split_axi...  8.81 us
    select_n x1, local copies, waits for them, and re-layouts, per_device(): jnp.where(side, extra_matrix[:, None], 0.0).reshape(-1, n_ep * capacity)  7.89 us
    all_to_all x1, starting transfers between devices, per_device(): lax.all_to_all(out.reshape(n_ep, capacity, width + half), 'ep', split_axi...  5.71 us
    select_n x1, other arithmetic, per_device(): jnp.where(side, extra_matrix[:, None], 0.0).reshape(-1, n_ep * capacity)  4.28 us
  transfers between devices with their start and end apart: 2, of which 2 were waited for; matrix products, arithmetic and copies ran while one was open for 9% of the time, Pallas kernels for 0%

profile of v1, /device:TPU:1, one launch (start us, length us, event | category | flops | bytes accessed | tf_op | source)
XLA Modules:
  0.0 175.1 jit_solution(12169227518639978864)
XLA Ops:
  0.0 0.8 copy.20
  0.9 0.3 convert_reduce_fusion
  1.2 0.8 compare_reduce_fusion
  1.9 0.8 fusion.13
  3.0 0.1 reduce_or.21
  3.1 0.5 fusion
  3.6 0.4 convolution_convert_fusion
  4.1 1.0 pad_maximum_fusion
  5.1 14.8 %all-to-all-start = ((bf16[64,8,768]{2,1,0:T(8,128)(2,1)}), bf16[64,8,768]{2,1,0:T(8,128)(2,1)S(1)}, u32[]{:S(2)}, u32[]{:S(2)}) async-start(bf16[64,8,768]{2,1,0:T(8,128)(2,1)} %pad_maximum_fusion), calls=%async_computation | async-start | bytes 1572864 | tf_op jit(solution)/shard_map/all_to_all | solution.py:278
  20.0 1.6 copy.27
  21.6 21.1 %all-to-all-done = bf16[64,8,768]{2,1,0:T(8,128)(2,1)S(1)} async-done(((bf16[64,8,768]{2,1,0:T(8,128)(2,1)}), bf16[64,8,768]{2,1,0:T(8,128)(2,1)S(1)}, u32[]{:S(2)}, u32[]{:S(2)}) %all-to-all-start) | async-done | bytes 786464 | tf_op jit(solution)/shard_map/all_to_all | solution.py:278
  42.7 0.9 copy-done.1
  43.6 101.5 %shard_map.91 = bf16[512,768]{1,0:T(8,128)(2,1)} custom-call(bf16[512,768]{1,0:T(8,128)(2,1)} %bitcast.32, bf16[4096,256]{1,0:T(8,128)(2,1)} %bitcast.26, bf16[128,4096]{1,0:T(8,128)(2,1)} %bitcast.38, bf16[1024,512]{1,0:T(8,128)(2,1)} %bitcast.39, bf16[512,512]{1,0:T(8,128)(2,1)} %bitcast.40), custom_call_target="tpu_custom_call" | custom-call | tf_op jit(solution)/shard_map/pallas_call | solution.py:222
  145.2 5.7 %all-to-all-start.1 = ((bf16[64,8,768]{2,1,0:T(8,128)(2,1)}), bf16[64,8,768]{2,1,0:T(8,128)(2,1)S(1)}, u32[]{:S(2)}, u32[]{:S(2)}) async-start(bf16[64,8,768]{2,1,0:T(8,128)(2,1)} %bitcast.31), calls=%async_computation.1 | async-start | bytes 1572864 | tf_op jit(solution)/shard_map/all_to_all | solution.py:282
  151.0 0.6 select_reduce_fusion
  151.6 0.1 copy.23
  151.7 0.9 copy.24
  152.7 4.3 %broadcast_select_fusion = f32[64,2,32,2,8]{4,3,2,1,0:T(2,128)} fusion(pred[2,2]{1,0:T(4,128)(4,1)S(1)} %iota_compare_fusion.2, f32[64,32,8]{2,1,0:T(8,128)S(1)} %copy.24), kind=kLoop, calls=%fused_computation | loop fusion | flops 65536 | bytes 327684 | tf_op jit(solution)/shard_map/jit(_where)/select_n | solution.py:291
  156.9 7.9 %select_n.43 = f32[128,512]{1,0:T(8,128)S(1)} reshape(f32[64,2,32,2,8]{4,3,2,1,0:T(2,128)} %broadcast_select_fusion) | data formatting | bytes 524288 | tf_op jit(solution)/shard_map/jit(_where)/select_n | solution.py:291
  164.8 8.8 %all-to-all-done.1 = bf16[64,8,768]{2,1,0:T(8,128)(2,1)S(1)} async-done(((bf16[64,8,768]{2,1,0:T(8,128)(2,1)}), bf16[64,8,768]{2,1,0:T(8,128)(2,1)S(1)}, u32[]{:S(2)}, u32[]{:S(2)}) %all-to-all-start.1) | async-done | bytes 786464 | tf_op jit(solution)/shard_map/all_to_all | solution.py:282
  173.6 0.2 fusion.5
  173.9 0.2 fusion.9
  174.1 0.2 convolution_add_fusion
  174.3 0.8 fusion.2
  (21 shorter events, 0.6 us)
Async XLA Ops:
  0.0 3.6 %copy-start = (bf16[64,512]{1,0:T(8,128)(2,1)S(1)}, bf16[64,512]{1,0:T(8,128)(2,1)}, u32[]{:S(2)}) copy-start(bf16[64,512]{1,0:T(8,128)(2,1)} %param.9) | copy-start | bytes 196612
  4.1 15.8 %copy-start.2 = (bf16[1,4096,2,128]{3,2,1,0:T(2,128)(2,1)S(1)}, bf16[1,4096,2,128]{3,2,1,0:T(2,128)(2,1)}, u32[]{:S(2)}) copy-start(bf16[1,4096,2,128]{3,2,1,0:T(2,128)(2,1)} %param.14) | copy-start | bytes 6291460
  5.1 37.6 %all-to-all-start = ((bf16[64,8,768]{2,1,0:T(8,128)(2,1)}), bf16[64,8,768]{2,1,0:T(8,128)(2,1)S(1)}, u32[]{:S(2)}, u32[]{:S(2)}) async-start(bf16[64,8,768]{2,1,0:T(8,128)(2,1)} %pad_maximum_fusion), calls=%async_computation | async-start | bytes 1572864 | tf_op jit(solution)/shard_map/all_to_all | solution.py:278
  42.7 0.9 copy-start.1
  145.2 5.7 %copy-start.3 = (f32[64,8]{0,1:T(8,128)S(1)}, f32[64,8]{0,1:T(8,128)}, u32[]{:S(2)}) copy-start(f32[64,8]{0,1:T(8,128)} %param.11) | copy-start | bytes 6148
  145.2 28.5 %all-to-all-start.1 = ((bf16[64,8,768]{2,1,0:T(8,128)(2,1)}), bf16[64,8,768]{2,1,0:T(8,128)(2,1)S(1)}, u32[]{:S(2)}, u32[]{:S(2)}) async-start(bf16[64,8,768]{2,1,0:T(8,128)(2,1)} %bitcast.31), calls=%async_computation.1 | async-start | bytes 1572864 | tf_op jit(solution)/shard_map/all_to_all | solution.py:282

commit v2 on v1

v2 whole, which is shorter than its diff:
```python
import functools

import jax
import jax.numpy as jnp
from jax import lax
from jax.experimental import pallas as pl
from jax.experimental.pallas import tpu as pltpu
from jax.sharding import PartitionSpec as P

MESH = pl.DeviceIdType.MESH
F32 = jnp.float32
BF16 = jnp.bfloat16
CHUNKS = 4
CW, CCW = 0, 1


def hops(chunk, way):
    return 4 if chunk % 2 == way else 3


def expert_kernel(
    tokens_ref, pairs_ref, wh_hbm, ws_hbm, dh_hbm, ds_hbm, out_ref,
    tok, tab, tab_sibling, send, mine, feat, pair_feat, hid, acc_h, acc_s, part, pair_part,
    out, back, combine, mix, mix_sibling, wh_ref, ws_ref, dh_ref, ds_ref, dspare,
    ring_send, ring_recv, pair_send, pair_recv, hid_send, hid_recv, part_send, part_recv,
    load_sem, swap_send, swap_recv, go_send, go_recv, own_sem, back_send, back_recv,
):
    n_dp, n_z, n_x = 8, 8, 4
    n_chips = n_z * n_x
    ep = lax.axis_index("ep")
    me = lax.axis_index("dp")
    core = lax.rem(ep, 2)
    chip = ep // 2
    at_x = lax.rem(chip, n_x)
    at_z = chip // n_x
    sibling = {"ep": ep + 1 - 2 * core, "dp": me}
    ring = (
        {"ep": ep, "dp": lax.rem(me + 1, n_dp)},
        {"ep": ep, "dp": lax.rem(me + n_dp - 1, n_dp)},
    )

    def chip_at(dx, dz):
        return lax.rem(at_z + dz, n_z) * n_x + lax.rem(at_x + dx, n_x)

    loads = [
        pltpu.make_async_copy(src, dst, load_sem.at[i])
        for i, (src, dst) in enumerate(
            ((wh_hbm, wh_ref), (ws_hbm, ws_ref), (dh_hbm, dh_ref), (ds_hbm, ds_ref))
        )
    ]
    for load in loads:
        load.start()

    barrier = pltpu.get_barrier_semaphore()
    for other in (sibling, ring[0], ring[1]):
        pl.semaphore_signal(barrier, inc=1, device_id=other, device_id_type=MESH)

    @pl.loop(1, n_chips)
    def _(step):
        other = lax.rem(chip + step, n_chips)
        pl.semaphore_signal(
            barrier, inc=1, device_id={"ep": other * 2 + core, "dp": me}, device_id_type=MESH
        )

    pl.semaphore_wait(barrier, n_chips + 2)

    group = tokens_ref.shape[0]
    width = tokens_ref.shape[1]
    half = width // 2
    block = 16
    rows = n_z * block
    units = wh_ref.shape[1] // 2

    swaps = [
        pltpu.make_async_remote_copy(
            src_ref=src, dst_ref=dst, send_sem=swap_send.at[i], recv_sem=swap_recv.at[i],
            device_id=sibling, device_id_type=MESH,
        )
        for i, (src, dst) in enumerate(
            ((tokens_ref, tok.at[pl.ds(core * group, group)]), (pairs_ref, tab_sibling))
        )
    ]
    for swap in swaps:
        swap.start()
    tok[pl.ds(pl.multiple_of(core * group, group), group), :] = tokens_ref[...]
    for swap in swaps:
        swap.wait_recv()

    both_tables = pairs_ref[...] + tab_sibling[...]
    top_k = pairs_ref.shape[0] // 2
    tab[...] = both_tables
    slot_rows = n_chips * block
    row = lax.broadcasted_iota(jnp.int32, (slot_rows, 2 * group), 0)
    of_group = row % block // 8 * 1024 + row % 8 + 1
    home_key = (of_group + (row // block * 2 + core) * 8).astype(F32)
    spare_key = (of_group + (row // block + 2 * n_chips) * 8).astype(F32)

    def spread(key, weighted):
        found = jnp.zeros(key.shape, F32)
        for k in range(top_k):
            value = tab[top_k + k : top_k + k + 1, :] if weighted else 1.0
            found += jnp.where(tab[k : k + 1, :] == key, value, 0.0)
        return found

    send[:, :width] = jnp.dot(
        spread(home_key, False).astype(BF16), tok[...], preferred_element_type=F32
    ).astype(BF16)
    send[:, width:] = jnp.dot(
        spread(spare_key, False).astype(BF16),
        tok[:, pl.ds(pl.multiple_of(core * half, half), half)],
        preferred_element_type=F32,
    ).astype(BF16)

    def go_copy(dx, dz):
        other = chip_at(dx, dz)
        return pltpu.make_async_remote_copy(
            src_ref=send.at[pl.ds(other * block, block)],
            dst_ref=mine.at[pl.ds((dx * n_z + at_z) * block, block)],
            send_sem=go_send, recv_sem=go_recv.at[dx],
            device_id={"ep": other * 2 + core, "dp": me}, device_id_type=MESH,
        )

    own_go = pltpu.make_async_copy(
        send.at[pl.ds(chip * block, block)], mine.at[pl.ds(at_z * block, block)], own_sem.at[0]
    )
    own_go.start()
    for dx in range(n_x):
        @pl.loop(0 if dx else 1, n_z)
        def _(dz):
            go_copy(dx, dz).start()

    def source(way, hop):
        return lax.rem(me + (n_dp - hop if way == CW else hop), n_dp)

    def feat_copy(chunk, way, hop):
        src = source(way, hop - 1)
        window = pl.ds(chunk * rows, rows)
        return pltpu.make_async_remote_copy(
            src_ref=mine.at[window] if hop == 1 else feat.at[src, window],
            dst_ref=feat.at[src, window],
            send_sem=ring_send.at[chunk, way, hop - 1],
            recv_sem=ring_recv.at[chunk, way, hop - 1],
            device_id=ring[way], device_id_type=MESH,
        )

    def pair_copy(chunk, way, hop):
        src = source(way, hop)
        window = pl.ds(chunk * rows, rows)
        here = mine.at[window, pl.ds(width, half)] if hop == 0 else feat.at[src, window, pl.ds(width, half)]
        return pltpu.make_async_remote_copy(
            src_ref=here,
            dst_ref=pair_feat.at[src, window],
            send_sem=pair_send.at[chunk, way, hop],
            recv_sem=pair_recv.at[chunk, way, hop],
            device_id=sibling, device_id_type=MESH,
        )

    hid_rows = rows + rows // 2

    def hid_copy(chunk, way, hop):
        src = source(way, hop - 1)
        window = pl.ds(chunk * hid_rows, hid_rows)
        return pltpu.make_async_remote_copy(
            src_ref=hid.at[src, window],
            dst_ref=hid.at[src, window],
            send_sem=hid_send.at[chunk, way, hop - 1],
            recv_sem=hid_recv.at[chunk, way, hop - 1],
            device_id=ring[way], device_id_type=MESH,
        )

    columns = ds_ref.shape[1]
    out_half = columns // 2

    def part_copy(chunk):
        window = pl.ds(chunk * rows, rows)
        return pltpu.make_async_remote_copy(
            src_ref=part.at[window, pl.ds((1 - core) * out_half, out_half)],
            dst_ref=pair_part.at[window],
            send_sem=part_send.at[chunk],
            recv_sem=part_recv.at[chunk],
            device_id=sibling, device_id_type=MESH,
        )

    def back_copy(dx, dz):
        z = lax.rem(at_z + dz, n_z)
        other = chip_at(n_x - dx, dz)
        return pltpu.make_async_remote_copy(
            src_ref=out.at[pl.ds((dx * n_z + z) * block, block)],
            dst_ref=back.at[pl.ds(chip * block, block)],
            send_sem=back_send, recv_sem=back_recv,
            device_id={"ep": other * 2 + core, "dp": me}, device_id_type=MESH,
        )

    turned_dims = (((1,), (1,)), ((), ()))

    def spare_term(x, at, side):
        cols = pl.ds(pl.multiple_of(at * width + side * half, half), half)
        return lax.dot_general(x, ws_ref[:, cols], turned_dims, preferred_element_type=F32)

    def project(x, at):
        w = wh_ref[pl.ds(pl.multiple_of(at * width, width), width), :]
        home = jnp.dot(x[:, :width], w, preferred_element_type=F32)
        return home, spare_term(x[:, width:], at, core)

    def begin(chunk):
        window = pl.ds(chunk * rows, rows)
        arrived = mine.at[pl.ds(chunk * rows, rows if chunk else rows - block)]
        pltpu.make_async_copy(arrived, arrived, go_recv.at[chunk]).wait()
        if chunk == 0:
            own_go.wait()
        for way in (CW, CCW):
            feat_copy(chunk, way, 1).start()
        pair_copy(chunk, CW, 0).start()
        if chunk == 0:
            loads[0].wait()
            loads[1].wait()
        acc_h[window, :], acc_s[window, :] = project(mine[window, :], me)

    def add_pair(chunk, way, hop):
        window = pl.ds(chunk * rows, rows)
        src = source(way, hop)
        pair_copy(chunk, way, hop).wait_recv()
        acc_s[window, :] += spare_term(pair_feat[src, window, :], src, 1 - core)

    def arrive(chunk, hop):
        window = pl.ds(chunk * rows, rows)
        ways = [way for way in (CW, CCW) if hop <= hops(chunk, way)]
        for way in ways:
            feat_copy(chunk, way, hop).wait_recv()
            if hop < hops(chunk, way):
                feat_copy(chunk, way, hop + 1).start()
            pair_copy(chunk, way, hop).start()
        for way in ways:
            src = source(way, hop)
            home, spare = project(feat[src, window, :], src)
            acc_h[window, :] += home
            acc_s[window, :] += spare
        if hop == 1:
            add_pair(chunk, CW, 0)
        else:
            for way in (CW, CCW):
                add_pair(chunk, way, hop - 1)

    def first_half(chunk):
        window = pl.ds(chunk * rows, rows)
        for way in (CW, CCW):
            if hops(chunk, way) == 4:
                add_pair(chunk, way, 4)
        gate = acc_h[window, :units]
        base = chunk * hid_rows
        hid[me, pl.ds(base, rows), :] = (gate / (1.0 + jnp.exp(-gate)) * acc_h[window, units:]).astype(BF16)
        plain = acc_s[window, :]
        turned = pltpu.roll(plain, units // 2, 1)
        low = lax.broadcasted_iota(jnp.int32, plain.shape, 1) < units // 2
        gate = jnp.where(low, plain, turned)
        both = gate / (1.0 + jnp.exp(-gate)) * jnp.where(low, turned, plain)
        top = rows // 2
        packed = jnp.where(low[:top], both[:top], both[top:])
        hid[me, pl.ds(base + rows, top), :] = packed.astype(BF16)
        for way in (CW, CCW):
            hid_copy(chunk, way, 1).start()

    def hid_arrive(chunk, hop):
        for way in (CW, CCW):
            if hop <= hops(chunk, way):
                hid_copy(chunk, way, hop).wait_recv()
                if hop < hops(chunk, way):
                    hid_copy(chunk, way, hop + 1).start()

    def second_half(chunk):
        window = pl.ds(chunk * rows, rows)
        base = chunk * hid_rows
        top = rows // 2
        packed = jnp.concatenate([hid[at, pl.ds(base + rows, top), :] for at in range(n_dp)], axis=1)
        low = lax.broadcasted_iota(jnp.int32, packed.shape, 1) % units < units // 2
        none = jnp.zeros_like(packed)
        both = jnp.concatenate([jnp.where(low, packed, none), jnp.where(low, none, packed)], axis=0)
        part[window, :] = jnp.dot(both, dspare[...], preferred_element_type=F32)
        part_copy(chunk).start()
        whole = jnp.concatenate([hid[at, pl.ds(base, rows), :] for at in range(n_dp)], axis=1)
        out[window, :columns] = jnp.dot(whole, dh_ref[...], preferred_element_type=F32).astype(BF16)

    own_back = pltpu.make_async_copy(
        out.at[pl.ds(at_z * block, block)], back.at[pl.ds(chip * block, block)], own_sem.at[1]
    )

    def finish(chunk):
        window = pl.ds(chunk * rows, rows)
        part_copy(chunk).wait_recv()
        own = part[window, pl.ds(pl.multiple_of(core * out_half, out_half), out_half)]
        out[window, columns:] = (own + pair_part[window, :]).astype(BF16)
        if chunk == 0:
            own_back.start()

        @pl.loop(0 if chunk else 1, n_z)
        def _(dz):
            back_copy(chunk, dz).start()

    def prepare():
        for i, key in enumerate((home_key, spare_key)):
            whole = spread(key, True).T
            high = whole.astype(BF16)
            combine[2 * i] = high
            combine[2 * i + 1] = (whole - high.astype(F32)).astype(BF16)
        loads[2].wait()
        loads[3].wait()
        for at in range(n_dp):
            w = ds_ref[pl.ds(at * units // 2, units // 2), :]
            dspare[pl.ds(at * units, units // 2), :] = w
            dspare[pl.ds(at * units + units // 2, units // 2), :] = w

    events = []
    for chunk in range(CHUNKS):
        for hop in range(5):
            events.append((chunk + hop, 0, -chunk, "feat", chunk, hop))
        events.append((chunk + 4, 1, -chunk, "first", chunk, 0))
        for hop in range(1, 5):
            events.append((chunk + 4 + hop, 2, -chunk, "hid", chunk, hop))
        events.append((chunk + 8, 3, -chunk, "second", chunk, 0))
        events.append((chunk + 9, 4, -chunk, "finish", chunk, 0))
    events.append((0, 9, 0, "prepare", 0, 0))
    for _, _, _, kind, chunk, hop in sorted(events):
        if kind == "feat":
            arrive(chunk, hop) if hop else begin(chunk)
        elif kind == "first":
            first_half(chunk)
        elif kind == "hid":
            hid_arrive(chunk, hop)
        elif kind == "second":
            second_half(chunk)
        elif kind == "finish":
            finish(chunk)
        else:
            prepare()

    landed = back.at[pl.ds(0, (n_chips - 1) * block)]
    pltpu.make_async_copy(landed, landed, back_recv).wait()
    own_back.wait()

    def weigh(i, table):
        return jnp.dot(combine[2 * i], table, preferred_element_type=F32) + jnp.dot(
            combine[2 * i + 1], table, preferred_element_type=F32
        )

    mix[...] = weigh(0, back[:, :columns])
    side = pl.ds(pl.multiple_of(core * out_half, out_half), out_half)
    mix[:, side] += weigh(1, back[:, columns:])
    mix_swap = pltpu.make_async_remote_copy(
        src_ref=mix.at[pl.ds((1 - core) * group, group)], dst_ref=mix_sibling,
        send_sem=swap_send.at[2], recv_sem=swap_recv.at[2],
        device_id=sibling, device_id_type=MESH,
    )
    mix_swap.start()
    mix_swap.wait_recv()
    out_ref[...] = (mix[pl.ds(pl.multiple_of(core * group, group), group), :] + mix_sibling[...]).astype(BF16)

    mix_swap.wait_send()
    for swap in swaps:
        swap.wait_send()
    gone = send.at[pl.ds(0, (n_chips - 1) * block)]
    pltpu.make_async_copy(gone, gone, go_send).wait()
    gone = out.at[pl.ds(0, (n_chips - 1) * block)]
    pltpu.make_async_copy(gone, gone, back_send).wait()
    for chunk in range(CHUNKS):
        for way in (CW, CCW):
            for hop in range(1, hops(chunk, way) + 1):
                feat_copy(chunk, way, hop).wait_send()
                hid_copy(chunk, way, hop).wait_send()
                pair_copy(chunk, way, hop).wait_send()
        pair_copy(chunk, CW, 0).wait_send()
        part_copy(chunk).wait_send()


def experts(tokens, pairs, wh, ws, dh, ds):
    group, width = tokens.shape
    n_dp = 8
    half = width // 2
    units = wh.shape[1] // 2
    total = 512
    columns = ds.shape[1]
    lanes = pairs.shape[1]
    dma = pltpu.SemaphoreType.DMA
    ring_sems = dma((CHUNKS, 2, 4))
    pair_sems = dma((CHUNKS, 2, 5))
    part_sems = dma((CHUNKS,))
    in_vmem = pl.BlockSpec(memory_space=pltpu.VMEM)
    in_hbm = pl.BlockSpec(memory_space=pl.ANY)
    return pl.pallas_call(
        expert_kernel,
        out_shape=jax.ShapeDtypeStruct((group, columns), BF16),
        in_specs=[in_vmem] * 2 + [in_hbm] * 4,
        out_specs=in_vmem,
        scratch_shapes=[
            pltpu.VMEM((2 * group, width), BF16),
            pltpu.VMEM(pairs.shape, F32),
            pltpu.VMEM(pairs.shape, F32),
            pltpu.VMEM((total, width + half), BF16),
            pltpu.VMEM((total, width + half), BF16),
            pltpu.VMEM((n_dp, total, width + half), BF16),
            pltpu.VMEM((n_dp, total, half), BF16),
            pltpu.VMEM((n_dp, total + total // 2, units), BF16),
            pltpu.VMEM((total, 2 * units), F32),
            pltpu.VMEM((total, units), F32),
            pltpu.VMEM((total, columns), F32),
            pltpu.VMEM((total, columns // 2), F32),
            pltpu.VMEM((total, columns + columns // 2), BF16),
            pltpu.VMEM((total, columns + columns // 2), BF16),
            pltpu.VMEM((4, lanes, total), BF16),
            pltpu.VMEM((lanes, columns), F32),
            pltpu.VMEM((group, columns), F32),
            pltpu.VMEM(wh.shape, BF16),
            pltpu.VMEM(ws.shape, BF16),
            pltpu.VMEM(dh.shape, BF16),
            pltpu.VMEM(ds.shape, BF16),
            pltpu.VMEM((n_dp * units, columns), BF16),
            ring_sems, ring_sems, pair_sems, pair_sems, ring_sems, ring_sems, part_sems, part_sems,
            dma((4,)), dma((3,)), dma((3,)), dma, dma((4,)), dma((2,)), dma, dma,
        ],
        compiler_params=pltpu.CompilerParams(
            collective_id=0, has_side_effects=True, vmem_limit_bytes=56 * 1024 * 1024
        ),
    )(tokens, pairs, wh, ws, dh, ds)


def route(expert_ids, placement, split_rows, slots, capacity):
    per_group = expert_ids.shape[0] * expert_ids.shape[1]
    chosen = expert_ids.reshape(per_group)
    ordinal = jnp.arange(per_group, dtype=jnp.int32)
    same = (chosen[:, None] == chosen[None, :]) & (ordinal[None, :] < ordinal[:, None])
    rank = jnp.sum(same.astype(jnp.int32), axis=1)
    match = chosen[:, None] == placement[None, :]
    hot = jnp.any(match, axis=1)
    copy = jnp.sum(jnp.where(match, jnp.arange(placement.shape[0], dtype=jnp.int32)[None, :], 0), axis=1)
    split = jnp.sum(jnp.where(match, split_rows[None, :], 0), axis=1)
    moved = hot & (rank >= split)
    slot = jnp.where(moved, slots + copy, chosen)
    position = jnp.where(moved, rank - split, rank)
    return jnp.where(position < capacity, slot * capacity + position, -1).reshape(expert_ids.shape)


def per_device(
    tokens, expert_ids, gate_logits, placement, split_rows,
    gate_up_weight, down_weight, spare_gate_up, spare_down,
):
    n_ep = lax.axis_size("ep")
    core = lax.axis_index("ep") % 2
    table_row = route(expert_ids, placement, split_rows, n_ep, 8).T
    score = jax.nn.sigmoid(gate_logits)
    weight = (2.5 * score / jnp.sum(score, axis=1, keepdims=True)).T
    coded = jnp.where(table_row >= 0, table_row + 1 + 1024 * core, 0).astype(F32)
    pairs = jnp.concatenate([coded, weight], axis=0)
    side = jnp.arange(2)[None, :, None] == core
    pairs = jnp.where(side, pairs[:, None, :], 0.0).reshape(pairs.shape[0], -1)
    wh = gate_up_weight[0].reshape(gate_up_weight.shape[1], -1)
    ws = jnp.transpose(spare_gate_up[0], (1, 2, 0)).reshape(-1, spare_gate_up.shape[1])
    return experts(tokens, pairs, wh, ws, down_weight[0], spare_down[0])


def solution(mesh):
    return jax.shard_map(
        per_device,
        mesh=mesh,
        in_specs=(
            P("ep", "dp"),
            P("ep", None),
            P("ep", None),
            P(),
            P(),
            P("ep", None, None, "dp"),
            P("ep", None, "dp"),
            P("ep", None, None, "dp"),
            P("ep", None, "dp"),
        ),
        out_specs=P("ep", "dp"),
        check_vma=False,
    )
```

time: 176 us -> 139 us (0.79)
  waiting for transfers between devices: 29.9 us -> 0 us
  Pallas kernels: 102 us -> 128 us
  starting transfers between devices: 20.5 us -> 0 us
  local copies, waits for them, and re-layouts: 12.9 us -> 6.22 us
  other arithmetic: 8.18 us -> 3.83 us
  matrix products: 1.84 us -> 0 us
    all_to_all x2 -> x0, waiting for transfers between devices: 29.9 us -> none  [the longest x1 21.1 us: per_device(): rows = lax.all_to_all(send, 'ep', split_axis=0, concat_axis=0, tiled=True)]
    pallas_call x1, Pallas kernels: 102 us -> 128 us  [experts(): pl.pallas_call(expert_kernel, out_shape=jax.ShapeDtypeStruct((group, colu...]
    all_to_all x2 -> x0, starting transfers between devices: 20.5 us -> none  [the longest x1 14.8 us: per_device(): rows = lax.all_to_all(send, 'ep', split_axis=0, concat_axis=0, tiled=True)]
    select_n x1 -> x0, local copies, waits for them, and re-layouts: 7.89 us -> none  [per_device(): jnp.where(side, extra_matrix[:, None], 0.0).reshape(-1, n_ep * capacity)]
    select_n x2 -> x1, other arithmetic: 4.3 us -> 0.61 us  [per_device(): pairs = jnp.where(side, pairs[:, None, :], 0.0).reshape(pairs.shape[0], -1)]
    unnamed x10 -> x3, local copies, waits for them, and re-layouts: 3.35 us -> 5.47 us
    dot_general x5 -> x0, matrix products: 1.84 us -> none  [the longest x2 1.03 us: exact_dot(): jnp.dot(low, b, preferred_element_type=F32)]
  transfers between devices with their start and end apart: 2 -> 0, of which waited for: 2 -> 0; matrix products, arithmetic and copies ran while one was open for 9% -> 0% of each run, Pallas kernels for 0% -> 0%
where the time goes in v2:
time: 139 us; the launch traced here: 138 us
  Pallas kernels  128 us (92%)
  local copies, waits for them, and re-layouts  6.22 us (4%)
  other arithmetic  3.83 us (3%)
    pallas_call x1, Pallas kernels, experts(): pl.pallas_call(expert_kernel, out_shape=jax.ShapeDtypeStruct((group, colu...  128 us
    unnamed x3, local copies, waits for them, and re-layouts  5.47 us

profile of v2, /device:TPU:1, one launch (start us, length us, event | category | flops | bytes accessed | tf_op | source)
XLA Modules:
  0.0 138.4 jit_solution(8242723624236357596)
XLA Ops:
  0.0 0.1 broadcast_in_dim.58
  0.1 0.1 broadcast_in_dim.59
  0.2 0.7 fusion.3
  0.9 0.7 divide_bitcast_fusion
  1.6 0.8 copy.17
  2.4 0.1 eq.43
  2.5 0.8 compare_reduce_fusion
  3.2 0.2 convert_reduce_fusion
  3.5 0.8 fusion.1
  4.2 0.1 reduce_or.12
  4.3 0.1 add.38
  4.4 0.1 reduce_sum.43
  4.5 0.1 reduce_sum.41
  4.6 0.1 copy.19
  4.7 0.1 broadcast_in_dim.66
  4.8 0.6 broadcast_select_fusion.pairs_ref
  5.4 3.2 %copy.22 = bf16[512,8,2,128]{3,1,2,0:T(8,128)(2,1)} copy(bf16[512,8,2,128]{3,2,1,0:T(2,128)(2,1)} %bitcast.17) | data formatting | bytes 4194304
  8.6 128.3 %shard_map.91 = bf16[64,512]{1,0:T(8,128)(2,1)} custom-call(bf16[64,512]{1,0:T(8,128)(2,1)} %tokens_ref.1, f32[16,128]{1,0:T(8,128)} %broadcast_select_fusion.pairs_ref, bf16[4096,256]{1,0:T(8,128)(2,1)} %bitcast.16, bf16[128,4096]{1,0:T(8,128)(2,1)} %bitcast.18, bf16[1024,512]{1,0:T(8,128)(2,1)} %bitcast.19, bf16[512,512]{1,0:T(8,128)(2,1)} %bitcast.20), custom_call_target="tpu_custom_call" | custom-call | tf_op jit(solution)/shard_map/pallas_call | solution.py:388
  137.0 1.5 %copy.24 = bf16[64,512]{1,0:T(8,128)(2,1)} copy(bf16[64,512]{1,0:T(8,128)(2,1)} %shard_map.91) | data formatting | bytes 131072
  (5 shorter events, 0.1 us)

commit v3 on v2

--- a/solution.py
+++ b/solution.py
@@ -11,6 +11,7 @@
 F32 = jnp.float32
 BF16 = jnp.bfloat16
 CHUNKS = 4
+EXTRA = 128
 CW, CCW = 0, 1
 
 
@@ -19,11 +20,12 @@
 
 
 def expert_kernel(
-    tokens_ref, pairs_ref, wh_hbm, ws_hbm, dh_hbm, ds_hbm, out_ref,
-    tok, tab, tab_sibling, send, mine, feat, pair_feat, hid, acc_h, acc_s, part, pair_part,
-    out, back, combine, mix, mix_sibling, wh_ref, ws_ref, dh_ref, ds_ref, dspare,
+    tokens_ref, ids_ref, logits_ref, placement_ref, split_ref, wh_hbm, ws_hbm, dh_hbm, ds_hbm, out_ref,
+    tok, tab, tab_sibling, tok_extra, send, send_extra, mine, mine_extra, feat, pair_feat, hid, acc_h, acc_s, part, pair_part,
+    out, back, combine, mix, mix_sibling, wh_raw, wide, wh_ref, wh_extra, ws_ref, dh_ref, ds_ref, dspare,
     ring_send, ring_recv, pair_send, pair_recv, hid_send, hid_recv, part_send, part_recv,
     load_sem, swap_send, swap_recv, go_send, go_recv, own_sem, back_send, back_recv,
+    peer_send, peer_recv, extra_send, extra_recv,
 ):
     n_dp, n_z, n_x = 8, 8, 4
     n_chips = n_z * n_x
@@ -45,15 +47,21 @@
     loads = [
         pltpu.make_async_copy(src, dst, load_sem.at[i])
         for i, (src, dst) in enumerate(
-            ((wh_hbm, wh_ref), (ws_hbm, ws_ref), (dh_hbm, dh_ref), (ds_hbm, ds_ref))
+            ((wh_hbm, wh_raw), (ws_hbm, ws_ref), (dh_hbm, dh_ref), (ds_hbm, ds_ref))
         )
     ]
     for load in loads:
         load.start()
 
     barrier = pltpu.get_barrier_semaphore()
-    for other in (sibling, ring[0], ring[1]):
-        pl.semaphore_signal(barrier, inc=1, device_id=other, device_id_type=MESH)
+    pl.semaphore_signal(barrier, inc=1, device_id=sibling, device_id_type=MESH)
+
+    def dp_peer(step):
+        return {"ep": ep, "dp": lax.rem(me + step, n_dp)}
+
+    @pl.loop(1, n_dp)
+    def _(step):
+        pl.semaphore_signal(barrier, inc=1, device_id=dp_peer(step), device_id_type=MESH)
 
     @pl.loop(1, n_chips)
     def _(step):
@@ -62,51 +70,119 @@
             barrier, inc=1, device_id={"ep": other * 2 + core, "dp": me}, device_id_type=MESH
         )
 
-    pl.semaphore_wait(barrier, n_chips + 2)
-
     group = tokens_ref.shape[0]
     width = tokens_ref.shape[1]
     half = width // 2
+    lean = width - EXTRA
     block = 16
     rows = n_z * block
-    units = wh_ref.shape[1] // 2
-
+    units = dh_hbm.shape[0] // n_dp
+    top_k = ids_ref.shape[0]
+    experts_ = 2 * n_chips
+    lanes = 2 * group
+    slot_rows = n_chips * block
+
+    score = 1.0 / (1.0 + jnp.exp(-logits_ref[...]))
+    weight = 2.5 * score / jnp.sum(score, axis=0, keepdims=True)
+    high = weight.astype(BF16).astype(F32)
+    stack = jnp.concatenate([ids_ref[...].astype(F32), high, weight - high], axis=0).astype(BF16)
+    place = lax.broadcasted_iota(jnp.int32, (group, lanes), 1) - core * group
+    spot = (place == lax.broadcasted_iota(jnp.int32, (group, lanes), 0)).astype(F32).astype(BF16)
+    stack = jnp.dot(stack, spot, preferred_element_type=F32)
+    row = lax.broadcasted_iota(jnp.int32, (experts_, lanes), 0)
+    lane = lax.broadcasted_iota(jnp.int32, (experts_, lanes), 1)
+    expert = row % n_chips * 2 + row // n_chips
+    here = lane // group == core
+    hit = jnp.zeros((experts_, lanes), F32)
+    high = jnp.zeros((experts_, lanes), F32)
+    rest = jnp.zeros((experts_, lanes), F32)
+    for k in range(top_k):
+        same = (stack[k : k + 1, :] == expert.astype(F32)) & here
+        hit += jnp.where(same, 1.0, 0.0)
+        high += jnp.where(same, stack[top_k + k : top_k + k + 1, :], 0.0)
+        rest += jnp.where(same, stack[2 * top_k + k : 2 * top_k + k + 1, :], 0.0)
+    earlier = lax.broadcasted_iota(jnp.int32, (lanes, lanes), 0) < lax.broadcasted_iota(jnp.int32, (lanes, lanes), 1)
+    rank = jnp.dot(hit.astype(BF16), earlier.astype(F32).astype(BF16), preferred_element_type=F32)
+    hot = jnp.zeros((experts_, lanes), F32)
+    split = jnp.zeros((experts_, lanes), F32)
+    spares = placement_ref.shape[0]
+    spare_row = lax.broadcasted_iota(jnp.int32, (spares, experts_), 0)
+    placed = jnp.zeros((spares, experts_), jnp.int32)
+    for r in range(spares):
+        chosen = expert == placement_ref[r]
+        hot += jnp.where(chosen, 1.0, 0.0)
+        split += jnp.where(chosen, split_ref[r].astype(F32), 0.0)
+        placed = jnp.where(spare_row == r, placement_ref[r], placed)
+    column = lax.broadcasted_iota(jnp.int32, (spares, experts_), 1)
+    match = (placed == column % n_chips * 2 + column // n_chips).astype(F32).astype(BF16)
+    moved = (hot > 0.0) & (rank >= split)
+    capacity = 8.0
+    home_code = jnp.where((hit > 0.0) & ~moved & (rank < capacity), rank + 1.0, 0.0)
+    over = rank - split
+    spare_code = jnp.where((hit > 0.0) & moved & (over < capacity), over + 1.0, 0.0)
+    for i, (table, given) in enumerate(((home_code, spare_code), (high, high), (rest, rest))):
+        base = i * (experts_ + spares)
+        tab[pl.ds(base, experts_), :] = table
+        tab[pl.ds(base + experts_, spares), :] = jnp.dot(match, given.astype(BF16), preferred_element_type=F32)
+
+    loads[0].wait()
+
+    @pl.loop(0, n_dp)
+    def _(at):
+        wide[...] = wh_raw[pl.ds(pl.multiple_of(at * 2 * width, 2 * width), 2 * width), :].astype(F32)
+        for j in range(2):
+            plain = wide[pl.ds(j, width, stride=2), :].astype(BF16)
+            wh_ref[pl.ds(pl.multiple_of(at * lean, EXTRA), lean), j * units : (j + 1) * units] = plain[:lean]
+            wh_extra[pl.ds(pl.multiple_of(at * EXTRA, EXTRA), EXTRA), j * units : (j + 1) * units] = plain[lean:]
+
+    pl.semaphore_wait(barrier, n_chips + n_dp - 1)
+
+    own_tokens = pl.ds(pl.multiple_of(core * group, group), group)
     swaps = [
         pltpu.make_async_remote_copy(
             src_ref=src, dst_ref=dst, send_sem=swap_send.at[i], recv_sem=swap_recv.at[i],
             device_id=sibling, device_id_type=MESH,
         )
-        for i, (src, dst) in enumerate(
-            ((tokens_ref, tok.at[pl.ds(core * group, group)]), (pairs_ref, tab_sibling))
-        )
+        for i, (src, dst) in enumerate(((tokens_ref, tok.at[own_tokens]), (tab, tab_sibling)))
     ]
     for swap in swaps:
         swap.start()
-    tok[pl.ds(pl.multiple_of(core * group, group), group), :] = tokens_ref[...]
+
+    def peer_copy(step):
+        return pltpu.make_async_remote_copy(
+            src_ref=tokens_ref.at[:, pl.ds(lean, EXTRA)],
+            dst_ref=tok_extra.at[me, own_tokens],
+            send_sem=peer_send, recv_sem=peer_recv,
+            device_id=dp_peer(step), device_id_type=MESH,
+        )
+
+    @pl.loop(1, n_dp)
+    def _(step):
+        peer_copy(step).start()
+
+    tok[own_tokens, :] = tokens_ref[...]
+    tok_extra[me, own_tokens, :] = tokens_ref[:, lean:]
     for swap in swaps:
         swap.wait_recv()
 
-    both_tables = pairs_ref[...] + tab_sibling[...]
-    top_k = pairs_ref.shape[0] // 2
-    tab[...] = both_tables
-    slot_rows = n_chips * block
-    row = lax.broadcasted_iota(jnp.int32, (slot_rows, 2 * group), 0)
-    of_group = row % block // 8 * 1024 + row % 8 + 1
-    home_key = (of_group + (row // block * 2 + core) * 8).astype(F32)
-    spare_key = (of_group + (row // block + 2 * n_chips) * 8).astype(F32)
-
-    def spread(key, weighted):
-        found = jnp.zeros(key.shape, F32)
-        for k in range(top_k):
-            value = tab[top_k + k : top_k + k + 1, :] if weighted else 1.0
-            found += jnp.where(tab[k : k + 1, :] == key, value, 0.0)
-        return found
-
-    send[:, :width] = jnp.dot(
-        spread(home_key, False).astype(BF16), tok[...], preferred_element_type=F32
-    ).astype(BF16)
-    send[:, width:] = jnp.dot(
-        spread(spare_key, False).astype(BF16),
+    row = lax.broadcasted_iota(jnp.int32, (slot_rows, lanes), 0)
+    lane = lax.broadcasted_iota(jnp.int32, (slot_rows, lanes), 1)
+    in_group = row % block // 8 == lane // group
+    wanted = (row % 8 + 1).astype(F32)
+
+    def spread(i, spare):
+        base = i * (experts_ + spares) + (experts_ if spare else core * n_chips)
+        window = pl.ds(pl.multiple_of(base, n_chips), n_chips)
+        table = tab[window, :] + tab_sibling[window, :]
+        return jnp.broadcast_to(table[:, None, :], (n_chips, block, lanes)).reshape(slot_rows, lanes)
+
+    def picked(spare):
+        return (spread(0, spare) == wanted) & in_group
+
+    home_pick = picked(False).astype(F32).astype(BF16)
+    send[:, :lean] = jnp.dot(home_pick, tok[:, :lean], preferred_element_type=F32).astype(BF16)
+    send[:, lean:] = jnp.dot(
+        picked(True).astype(F32).astype(BF16),
         tok[:, pl.ds(pl.multiple_of(core * half, half), half)],
         preferred_element_type=F32,
     ).astype(BF16)
@@ -129,6 +205,39 @@
         def _(dz):
             go_copy(dx, dz).start()
 
+    peers_in = tok_extra.at[pl.ds(0, n_dp - 1), pl.ds(0, group)]
+    pltpu.make_async_copy(peers_in, peers_in, peer_recv).wait()
+    extra_swap = pltpu.make_async_remote_copy(
+        src_ref=tok_extra.at[:, own_tokens], dst_ref=tok_extra.at[:, own_tokens],
+        send_sem=swap_send.at[3], recv_sem=swap_recv.at[3], device_id=sibling, device_id_type=MESH,
+    )
+    extra_swap.start()
+
+    def extra_copy(dx, dz):
+        other = chip_at(dx, dz)
+        return pltpu.make_async_remote_copy(
+            src_ref=send_extra.at[pl.ds(other * block, block)],
+            dst_ref=mine_extra.at[pl.ds((dx * n_z + at_z) * block, block)],
+            send_sem=extra_send, recv_sem=extra_recv.at[dx],
+            device_id={"ep": other * 2 + core, "dp": me}, device_id_type=MESH,
+        )
+
+    own_extra = pltpu.make_async_copy(
+        send_extra.at[pl.ds(chip * block, block)], mine_extra.at[pl.ds(at_z * block, block)], own_sem.at[2]
+    )
+
+    def send_extras():
+        extra_swap.wait_recv()
+        for at in range(n_dp):
+            send_extra[:, at * EXTRA : (at + 1) * EXTRA] = jnp.dot(
+                home_pick, tok_extra[at], preferred_element_type=F32
+            ).astype(BF16)
+        own_extra.start()
+        for dx in range(n_x):
+            @pl.loop(0 if dx else 1, n_z)
+            def _(dz):
+                extra_copy(dx, dz).start()
+
     def source(way, hop):
         return lax.rem(me + (n_dp - hop if way == CW else hop), n_dp)
 
@@ -146,7 +255,7 @@
     def pair_copy(chunk, way, hop):
         src = source(way, hop)
         window = pl.ds(chunk * rows, rows)
-        here = mine.at[window, pl.ds(width, half)] if hop == 0 else feat.at[src, window, pl.ds(width, half)]
+        here = mine.at[window, pl.ds(lean, half)] if hop == 0 else feat.at[src, window, pl.ds(lean, half)]
         return pltpu.make_async_remote_copy(
             src_ref=here,
             dst_ref=pair_feat.at[src, window],
@@ -198,9 +307,9 @@
         return lax.dot_general(x, ws_ref[:, cols], turned_dims, preferred_element_type=F32)
 
     def project(x, at):
-        w = wh_ref[pl.ds(pl.multiple_of(at * width, width), width), :]
-        home = jnp.dot(x[:, :width], w, preferred_element_type=F32)
-        return home, spare_term(x[:, width:], at, core)
+        w = wh_ref[pl.ds(pl.multiple_of(at * lean, EXTRA), lean), :]
+        home = jnp.dot(x[:, :lean], w, preferred_element_type=F32)
+        return home, spare_term(x[:, lean:], at, core)
 
     def begin(chunk):
         window = pl.ds(chunk * rows, rows)
@@ -212,7 +321,6 @@
             feat_copy(chunk, way, 1).start()
         pair_copy(chunk, CW, 0).start()
         if chunk == 0:
-            loads[0].wait()
             loads[1].wait()
         acc_h[window, :], acc_s[window, :] = project(mine[window, :], me)
 
@@ -246,6 +354,11 @@
         for way in (CW, CCW):
             if hops(chunk, way) == 4:
                 add_pair(chunk, way, 4)
+        came = mine_extra.at[pl.ds(chunk * rows, rows if chunk else rows - block)]
+        pltpu.make_async_copy(came, came, extra_recv.at[chunk]).wait()
+        if chunk == 0:
+            own_extra.wait()
+        acc_h[window, :] += jnp.dot(mine_extra[window, :], wh_extra[...], preferred_element_type=F32)
         gate = acc_h[window, :units]
         base = chunk * hid_rows
         hid[me, pl.ds(base, rows), :] = (gate / (1.0 + jnp.exp(-gate)) * acc_h[window, units:]).astype(BF16)
@@ -297,11 +410,9 @@
             back_copy(chunk, dz).start()
 
     def prepare():
-        for i, key in enumerate((home_key, spare_key)):
-            whole = spread(key, True).T
-            high = whole.astype(BF16)
-            combine[2 * i] = high
-            combine[2 * i + 1] = (whole - high.astype(F32)).astype(BF16)
+        for i, spare in enumerate((False, True)):
+            for j in range(2):
+                combine[2 * i + j] = jnp.where(picked(spare), spread(1 + j, spare), 0.0).T.astype(BF16)
         loads[2].wait()
         loads[3].wait()
         for at in range(n_dp):
@@ -319,6 +430,7 @@
         events.append((chunk + 8, 3, -chunk, "second", chunk, 0))
         events.append((chunk + 9, 4, -chunk, "finish", chunk, 0))
     events.append((0, 9, 0, "prepare", 0, 0))
+    events.append((0, 0, 9, "extra", 0, 0))
     for _, _, _, kind, chunk, hop in sorted(events):
         if kind == "feat":
             arrive(chunk, hop) if hop else begin(chunk)
@@ -330,6 +442,8 @@
             second_half(chunk)
         elif kind == "finish":
             finish(chunk)
+        elif kind == "extra":
+            send_extras()
         else:
             prepare()
 
@@ -355,6 +469,10 @@
     out_ref[...] = (mix[pl.ds(pl.multiple_of(core * group, group), group), :] + mix_sibling[...]).astype(BF16)
 
     mix_swap.wait_send()
+    extra_swap.wait_send()
+    pltpu.make_async_copy(peers_in, peers_in, peer_send).wait()
+    gone = send_extra.at[pl.ds(0, (n_chips - 1) * block)]
+    pltpu.make_async_copy(gone, gone, extra_send).wait()
     for swap in swaps:
         swap.wait_send()
     gone = send.at[pl.ds(0, (n_chips - 1) * block)]
@@ -371,32 +489,38 @@
         part_copy(chunk).wait_send()
 
 
-def experts(tokens, pairs, wh, ws, dh, ds):
+def experts(tokens, ids, logits, placement, split_rows, wh, ws, dh, ds):
     group, width = tokens.shape
     n_dp = 8
     half = width // 2
-    units = wh.shape[1] // 2
+    lean = width - EXTRA
+    units = wh.shape[1]
     total = 512
     columns = ds.shape[1]
-    lanes = pairs.shape[1]
+    lanes = 2 * group
+    table_rows = 3 * (64 + placement.shape[0])
     dma = pltpu.SemaphoreType.DMA
     ring_sems = dma((CHUNKS, 2, 4))
     pair_sems = dma((CHUNKS, 2, 5))
     part_sems = dma((CHUNKS,))
     in_vmem = pl.BlockSpec(memory_space=pltpu.VMEM)
+    in_smem = pl.BlockSpec(memory_space=pltpu.SMEM)
     in_hbm = pl.BlockSpec(memory_space=pl.ANY)
     return pl.pallas_call(
         expert_kernel,
         out_shape=jax.ShapeDtypeStruct((group, columns), BF16),
-        in_specs=[in_vmem] * 2 + [in_hbm] * 4,
+        in_specs=[in_vmem] * 3 + [in_smem] * 2 + [in_hbm] * 4,
         out_specs=in_vmem,
         scratch_shapes=[
-            pltpu.VMEM((2 * group, width), BF16),
-            pltpu.VMEM(pairs.shape, F32),
-            pltpu.VMEM(pairs.shape, F32),
-            pltpu.VMEM((total, width + half), BF16),
-            pltpu.VMEM((total, width + half), BF16),
-            pltpu.VMEM((n_dp, total, width + half), BF16),
+            pltpu.VMEM((lanes, width), BF16),
+            pltpu.VMEM((table_rows, lanes), F32),
+            pltpu.VMEM((table_rows, lanes), F32),
+            pltpu.VMEM((n_dp, lanes, EXTRA), BF16),
+            pltpu.VMEM((total, lean + half), BF16),
+            pltpu.VMEM((total, n_dp * EXTRA), BF16),
+            pltpu.VMEM((total, lean + half), BF16),
+            pltpu.VMEM((total, n_dp * EXTRA), BF16),
+            pltpu.VMEM((n_dp, total, lean + half), BF16),
             pltpu.VMEM((n_dp, total, half), BF16),
             pltpu.VMEM((n_dp, total + total // 2, units), BF16),
             pltpu.VMEM((total, 2 * units), F32),
@@ -409,51 +533,32 @@
             pltpu.VMEM((lanes, columns), F32),
             pltpu.VMEM((group, columns), F32),
             pltpu.VMEM(wh.shape, BF16),
+            pltpu.VMEM((2 * width, units), F32),
+            pltpu.VMEM((n_dp * lean, 2 * units), BF16),
+            pltpu.VMEM((n_dp * EXTRA, 2 * units), BF16),
             pltpu.VMEM(ws.shape, BF16),
             pltpu.VMEM(dh.shape, BF16),
             pltpu.VMEM(ds.shape, BF16),
             pltpu.VMEM((n_dp * units, columns), BF16),
             ring_sems, ring_sems, pair_sems, pair_sems, ring_sems, ring_sems, part_sems, part_sems,
-            dma((4,)), dma((3,)), dma((3,)), dma, dma((4,)), dma((2,)), dma, dma,
+            dma((4,)), dma((4,)), dma((4,)), dma, dma((4,)), dma((3,)), dma, dma,
+            dma, dma, dma, dma((4,)),
         ],
         compiler_params=pltpu.CompilerParams(
             collective_id=0, has_side_effects=True, vmem_limit_bytes=56 * 1024 * 1024
         ),
-    )(tokens, pairs, wh, ws, dh, ds)
-
-
-def route(expert_ids, placement, split_rows, slots, capacity):
-    per_group = expert_ids.shape[0] * expert_ids.shape[1]
-    chosen = expert_ids.reshape(per_group)
-    ordinal = jnp.arange(per_group, dtype=jnp.int32)
-    same = (chosen[:, None] == chosen[None, :]) & (ordinal[None, :] < ordinal[:, None])
-    rank = jnp.sum(same.astype(jnp.int32), axis=1)
-    match = chosen[:, None] == placement[None, :]
-    hot = jnp.any(match, axis=1)
-    copy = jnp.sum(jnp.where(match, jnp.arange(placement.shape[0], dtype=jnp.int32)[None, :], 0), axis=1)
-    split = jnp.sum(jnp.where(match, split_rows[None, :], 0), axis=1)
-    moved = hot & (rank >= split)
-    slot = jnp.where(moved, slots + copy, chosen)
-    position = jnp.where(moved, rank - split, rank)
-    return jnp.where(position < capacity, slot * capacity + position, -1).reshape(expert_ids.shape)
+    )(tokens, ids, logits, placement, split_rows, wh, ws, dh, ds)
 
 
 def per_device(
     tokens, expert_ids, gate_logits, placement, split_rows,
     gate_up_weight, down_weight, spare_gate_up, spare_down,
 ):
-    n_ep = lax.axis_size("ep")
-    core = lax.axis_index("ep") % 2
-    table_row = route(expert_ids, placement, split_rows, n_ep, 8).T
-    score = jax.nn.sigmoid(gate_logits)
-    weight = (2.5 * score / jnp.sum(score, axis=1, keepdims=True)).T
-    coded = jnp.where(table_row >= 0, table_row + 1 + 1024 * core, 0).astype(F32)
-    pairs = jnp.concatenate([coded, weight], axis=0)
-    side = jnp.arange(2)[None, :, None] == core
-    pairs = jnp.where(side, pairs[:, None, :], 0.0).reshape(pairs.shape[0], -1)
-    wh = gate_up_weight[0].reshape(gate_up_weight.shape[1], -1)
+    wh = gate_up_weight.reshape(-1, gate_up_weight.shape[3])
     ws = jnp.transpose(spare_gate_up[0], (1, 2, 0)).reshape(-1, spare_gate_up.shape[1])
-    return experts(tokens, pairs, wh, ws, down_weight[0], spare_down[0])
+    return experts(
+        tokens, expert_ids.T, gate_logits.T, placement, split_rows, wh, ws, down_weight[0], spare_down[0]
+    )
 
 
 def solution(mesh):

time: 139 us -> 119 us (0.86)
  Pallas kernels: 128 us -> 118 us
  local copies, waits for them, and re-layouts: 6.22 us -> 1.47 us
  other arithmetic: 3.83 us -> 0 us
    pallas_call x1, Pallas kernels: 128 us -> 118 us  [experts(): pl.pallas_call(expert_kernel, out_shape=jax.ShapeDtypeStruct((group, colu...]
    unnamed x3 -> x1, local copies, waits for them, and re-layouts: 5.47 us -> 1.47 us
    reduce_sum x3 -> x0, other arithmetic: 1.72 us -> none  [the longest x1 0.77 us: route(): split = jnp.sum(jnp.where(match, split_rows[None, :], 0), axis=1)]
where the time goes in v3:
time: 119 us
  Pallas kernels  118 us (99%)
  local copies, waits for them, and re-layouts  1.47 us (1%)
    pallas_call x1, Pallas kernels, experts(): pl.pallas_call(expert_kernel, out_shape=jax.ShapeDtypeStruct((group, colu...  118 us

profile of v3, /device:TPU:1, one launch (start us, length us, event | category | flops | bytes accessed | tf_op | source)
XLA Modules:
  0.0 119.0 jit_solution(4139900302338726443)
XLA Ops:
  0.0 117.5 %shard_map.91 = bf16[64,512]{1,0:T(8,128)(2,1)} custom-call(bf16[64,512]{1,0:T(8,128)(2,1)} %tokens_ref.1, s32[8,64]{1,0:T(8,128)} %bitcast.14, f32[8,64]{1,0:T(8,128)} %bitcast.15, s32[32]{0:T(128)} %placement_ref.1, s32[32]{0:T(128)} %split_ref.1, bf16[8192,128]{1,0:T(8,128)(2,1)} %bitcast.10, bf16[128,4096]{1,0:T(8,128)(2,1)} %bitcast.11, ...), custom_call_target="tpu_custom_call" | custom-call | tf_op jit(solution)/shard_map/pallas_call | solution.py:509
  117.5 1.5 %copy.11 = bf16[64,512]{1,0:T(8,128)(2,1)} copy(bf16[64,512]{1,0:T(8,128)(2,1)} %shard_map.91) | data formatting | bytes 131072

commit v4 on v3

--- a/solution.py
+++ b/solution.py
@@ -11,7 +11,12 @@
 F32 = jnp.float32
 BF16 = jnp.bfloat16
 CHUNKS = 4
-EXTRA = 128
+PART = 128
+EXTRA = 2 * PART
+
+
+def parts(chunk):
+    return 1 if chunk < 2 else 2
 CW, CCW = 0, 1
 
 
@@ -73,8 +78,17 @@
     group = tokens_ref.shape[0]
     width = tokens_ref.shape[1]
     half = width // 2
-    lean = width - EXTRA
     block = 16
+
+    def home_width(chunk):
+        return width - parts(chunk) * PART
+
+    def ring_width(chunk):
+        return half + home_width(chunk)
+
+    def extra_width(chunk):
+        return parts(chunk) * n_dp * PART
+
     rows = n_z * block
     units = dh_hbm.shape[0] // n_dp
     top_k = ids_ref.shape[0]
@@ -132,8 +146,12 @@
         wide[...] = wh_raw[pl.ds(pl.multiple_of(at * 2 * width, 2 * width), 2 * width), :].astype(F32)
         for j in range(2):
             plain = wide[pl.ds(j, width, stride=2), :].astype(BF16)
-            wh_ref[pl.ds(pl.multiple_of(at * lean, EXTRA), lean), j * units : (j + 1) * units] = plain[:lean]
-            wh_extra[pl.ds(pl.multiple_of(at * EXTRA, EXTRA), EXTRA), j * units : (j + 1) * units] = plain[lean:]
+            wh_ref[pl.ds(pl.multiple_of(at * width, width), width), j * units : (j + 1) * units] = plain
+            for part_at in range(2):
+                end = width - part_at * PART
+                wh_extra[part_at, pl.ds(pl.multiple_of(at * PART, PART), PART), j * units : (j + 1) * units] = (
+                    plain[end - PART : end]
+                )
 
     pl.semaphore_wait(barrier, n_chips + n_dp - 1)
 
@@ -150,7 +168,7 @@
 
     def peer_copy(step):
         return pltpu.make_async_remote_copy(
-            src_ref=tokens_ref.at[:, pl.ds(lean, EXTRA)],
+            src_ref=tokens_ref.at[:, pl.ds(width - EXTRA, EXTRA)],
             dst_ref=tok_extra.at[me, own_tokens],
             send_sem=peer_send, recv_sem=peer_recv,
             device_id=dp_peer(step), device_id_type=MESH,
@@ -161,7 +179,7 @@
         peer_copy(step).start()
 
     tok[own_tokens, :] = tokens_ref[...]
-    tok_extra[me, own_tokens, :] = tokens_ref[:, lean:]
+    tok_extra[me, own_tokens, :] = tokens_ref[:, width - EXTRA :]
     for swap in swaps:
         swap.wait_recv()
 
@@ -180,8 +198,9 @@
         return (spread(0, spare) == wanted) & in_group
 
     home_pick = picked(False).astype(F32).astype(BF16)
-    send[:, :lean] = jnp.dot(home_pick, tok[:, :lean], preferred_element_type=F32).astype(BF16)
-    send[:, lean:] = jnp.dot(
+    widest = home_width(0)
+    send[:, half:] = jnp.dot(home_pick, tok[:, :widest], preferred_element_type=F32).astype(BF16)
+    send[:, :half] = jnp.dot(
         picked(True).astype(F32).astype(BF16),
         tok[:, pl.ds(pl.multiple_of(core * half, half), half)],
         preferred_element_type=F32,
@@ -190,14 +209,16 @@
     def go_copy(dx, dz):
         other = chip_at(dx, dz)
         return pltpu.make_async_remote_copy(
-            src_ref=send.at[pl.ds(other * block, block)],
-            dst_ref=mine.at[pl.ds((dx * n_z + at_z) * block, block)],
-            send_sem=go_send, recv_sem=go_recv.at[dx],
+            src_ref=send.at[pl.ds(other * block, block), pl.ds(0, ring_width(dx))],
+            dst_ref=mine.at[pl.ds((dx * n_z + at_z) * block, block), pl.ds(0, ring_width(dx))],
+            send_sem=go_send.at[dx], recv_sem=go_recv.at[dx],
             device_id={"ep": other * 2 + core, "dp": me}, device_id_type=MESH,
         )
 
     own_go = pltpu.make_async_copy(
-        send.at[pl.ds(chip * block, block)], mine.at[pl.ds(at_z * block, block)], own_sem.at[0]
+        send.at[pl.ds(chip * block, block), pl.ds(0, ring_width(0))],
+        mine.at[pl.ds(at_z * block, block), pl.ds(0, ring_width(0))],
+        own_sem.at[0],
     )
     own_go.start()
     for dx in range(n_x):
@@ -206,32 +227,36 @@
             go_copy(dx, dz).start()
 
     peers_in = tok_extra.at[pl.ds(0, n_dp - 1), pl.ds(0, group)]
-    pltpu.make_async_copy(peers_in, peers_in, peer_recv).wait()
     extra_swap = pltpu.make_async_remote_copy(
         src_ref=tok_extra.at[:, own_tokens], dst_ref=tok_extra.at[:, own_tokens],
         send_sem=swap_send.at[3], recv_sem=swap_recv.at[3], device_id=sibling, device_id_type=MESH,
     )
-    extra_swap.start()
+
+    def swap_extras():
+        pltpu.make_async_copy(peers_in, peers_in, peer_recv).wait()
+        extra_swap.start()
 
     def extra_copy(dx, dz):
         other = chip_at(dx, dz)
         return pltpu.make_async_remote_copy(
-            src_ref=send_extra.at[pl.ds(other * block, block)],
-            dst_ref=mine_extra.at[pl.ds((dx * n_z + at_z) * block, block)],
-            send_sem=extra_send, recv_sem=extra_recv.at[dx],
+            src_ref=send_extra.at[pl.ds(other * block, block), pl.ds(0, extra_width(dx))],
+            dst_ref=mine_extra.at[pl.ds((dx * n_z + at_z) * block, block), pl.ds(0, extra_width(dx))],
+            send_sem=extra_send.at[dx], recv_sem=extra_recv.at[dx],
             device_id={"ep": other * 2 + core, "dp": me}, device_id_type=MESH,
         )
 
     own_extra = pltpu.make_async_copy(
-        send_extra.at[pl.ds(chip * block, block)], mine_extra.at[pl.ds(at_z * block, block)], own_sem.at[2]
+        send_extra.at[pl.ds(chip * block, block), pl.ds(0, extra_width(0))],
+        mine_extra.at[pl.ds(at_z * block, block), pl.ds(0, extra_width(0))],
+        own_sem.at[2],
     )
 
     def send_extras():
         extra_swap.wait_recv()
         for at in range(n_dp):
-            send_extra[:, at * EXTRA : (at + 1) * EXTRA] = jnp.dot(
-                home_pick, tok_extra[at], preferred_element_type=F32
-            ).astype(BF16)
+            both = jnp.dot(home_pick, tok_extra[at], preferred_element_type=F32).astype(BF16)
+            send_extra[:, at * PART : (at + 1) * PART] = both[:, PART:]
+            send_extra[:, (n_dp + at) * PART : (n_dp + at + 1) * PART] = both[:, :PART]
         own_extra.start()
         for dx in range(n_x):
             @pl.loop(0 if dx else 1, n_z)
@@ -244,9 +269,10 @@
     def feat_copy(chunk, way, hop):
         src = source(way, hop - 1)
         window = pl.ds(chunk * rows, rows)
-        return pltpu.make_async_remote_copy(
-            src_ref=mine.at[window] if hop == 1 else feat.at[src, window],
-            dst_ref=feat.at[src, window],
+        cols = pl.ds(0, ring_width(chunk))
+        return pltpu.make_async_remote_copy(
+            src_ref=mine.at[window, cols] if hop == 1 else feat.at[src, window, cols],
+            dst_ref=feat.at[src, window, cols],
             send_sem=ring_send.at[chunk, way, hop - 1],
             recv_sem=ring_recv.at[chunk, way, hop - 1],
             device_id=ring[way], device_id_type=MESH,
@@ -255,7 +281,7 @@
     def pair_copy(chunk, way, hop):
         src = source(way, hop)
         window = pl.ds(chunk * rows, rows)
-        here = mine.at[window, pl.ds(lean, half)] if hop == 0 else feat.at[src, window, pl.ds(lean, half)]
+        here = mine.at[window, pl.ds(0, half)] if hop == 0 else feat.at[src, window, pl.ds(0, half)]
         return pltpu.make_async_remote_copy(
             src_ref=here,
             dst_ref=pair_feat.at[src, window],
@@ -307,13 +333,14 @@
         return lax.dot_general(x, ws_ref[:, cols], turned_dims, preferred_element_type=F32)
 
     def project(x, at):
-        w = wh_ref[pl.ds(pl.multiple_of(at * lean, EXTRA), lean), :]
-        home = jnp.dot(x[:, :lean], w, preferred_element_type=F32)
-        return home, spare_term(x[:, lean:], at, core)
+        depth = x.shape[1] - half
+        w = wh_ref[pl.ds(pl.multiple_of(at * width, width), depth), :]
+        home = jnp.dot(x[:, half:], w, preferred_element_type=F32)
+        return home, spare_term(x[:, :half], at, core)
 
     def begin(chunk):
         window = pl.ds(chunk * rows, rows)
-        arrived = mine.at[pl.ds(chunk * rows, rows if chunk else rows - block)]
+        arrived = mine.at[pl.ds(chunk * rows, rows if chunk else rows - block), pl.ds(0, ring_width(chunk))]
         pltpu.make_async_copy(arrived, arrived, go_recv.at[chunk]).wait()
         if chunk == 0:
             own_go.wait()
@@ -322,7 +349,7 @@
         pair_copy(chunk, CW, 0).start()
         if chunk == 0:
             loads[1].wait()
-        acc_h[window, :], acc_s[window, :] = project(mine[window, :], me)
+        acc_h[window, :], acc_s[window, :] = project(mine[window, : ring_width(chunk)], me)
 
     def add_pair(chunk, way, hop):
         window = pl.ds(chunk * rows, rows)
@@ -340,7 +367,7 @@
             pair_copy(chunk, way, hop).start()
         for way in ways:
             src = source(way, hop)
-            home, spare = project(feat[src, window, :], src)
+            home, spare = project(feat[src, window, : ring_width(chunk)], src)
             acc_h[window, :] += home
             acc_s[window, :] += spare
         if hop == 1:
@@ -354,11 +381,13 @@
         for way in (CW, CCW):
             if hops(chunk, way) == 4:
                 add_pair(chunk, way, 4)
-        came = mine_extra.at[pl.ds(chunk * rows, rows if chunk else rows - block)]
+        came = mine_extra.at[pl.ds(chunk * rows, rows if chunk else rows - block), pl.ds(0, extra_width(chunk))]
         pltpu.make_async_copy(came, came, extra_recv.at[chunk]).wait()
         if chunk == 0:
             own_extra.wait()
-        acc_h[window, :] += jnp.dot(mine_extra[window, :], wh_extra[...], preferred_element_type=F32)
+        for part_at in range(parts(chunk)):
+            x = mine_extra[window, part_at * n_dp * PART : (part_at + 1) * n_dp * PART]
+            acc_h[window, :] += jnp.dot(x, wh_extra[part_at], preferred_element_type=F32)
         gate = acc_h[window, :units]
         base = chunk * hid_rows
         hid[me, pl.ds(base, rows), :] = (gate / (1.0 + jnp.exp(-gate)) * acc_h[window, units:]).astype(BF16)
@@ -430,7 +459,8 @@
         events.append((chunk + 8, 3, -chunk, "second", chunk, 0))
         events.append((chunk + 9, 4, -chunk, "finish", chunk, 0))
     events.append((0, 9, 0, "prepare", 0, 0))
-    events.append((0, 0, 9, "extra", 0, 0))
+    events.append((0, 0, 9, "peers", 0, 0))
+    events.append((1, 0, -0.5, "extra", 0, 0))
     for _, _, _, kind, chunk, hop in sorted(events):
         if kind == "feat":
             arrive(chunk, hop) if hop else begin(chunk)
@@ -444,6 +474,8 @@
             finish(chunk)
         elif kind == "extra":
             send_extras()
+        elif kind == "peers":
+            swap_extras()
         else:
             prepare()
 
@@ -471,12 +503,14 @@
     mix_swap.wait_send()
     extra_swap.wait_send()
     pltpu.make_async_copy(peers_in, peers_in, peer_send).wait()
-    gone = send_extra.at[pl.ds(0, (n_chips - 1) * block)]
-    pltpu.make_async_copy(gone, gone, extra_send).wait()
+    for chunk in range(CHUNKS):
+        count = rows if chunk else rows - block
+        gone = send_extra.at[pl.ds(0, count), pl.ds(0, extra_width(chunk))]
+        pltpu.make_async_copy(gone, gone, extra_send.at[chunk]).wait()
+        gone = send.at[pl.ds(0, count), pl.ds(0, ring_width(chunk))]
+        pltpu.make_async_copy(gone, gone, go_send.at[chunk]).wait()
     for swap in swaps:
         swap.wait_send()
-    gone = send.at[pl.ds(0, (n_chips - 1) * block)]
-    pltpu.make_async_copy(gone, gone, go_send).wait()
     gone = out.at[pl.ds(0, (n_chips - 1) * block)]
     pltpu.make_async_copy(gone, gone, back_send).wait()
     for chunk in range(CHUNKS):
@@ -493,7 +527,7 @@
     group, width = tokens.shape
     n_dp = 8
     half = width // 2
-    lean = width - EXTRA
+    lean = width - PART
     units = wh.shape[1]
     total = 512
     columns = ds.shape[1]
@@ -534,15 +568,15 @@
             pltpu.VMEM((group, columns), F32),
             pltpu.VMEM(wh.shape, BF16),
             pltpu.VMEM((2 * width, units), F32),
-            pltpu.VMEM((n_dp * lean, 2 * units), BF16),
-            pltpu.VMEM((n_dp * EXTRA, 2 * units), BF16),
+            pltpu.VMEM((n_dp * width, 2 * units), BF16),
+            pltpu.VMEM((2, n_dp * PART, 2 * units), BF16),
             pltpu.VMEM(ws.shape, BF16),
             pltpu.VMEM(dh.shape, BF16),
             pltpu.VMEM(ds.shape, BF16),
             pltpu.VMEM((n_dp * units, columns), BF16),
             ring_sems, ring_sems, pair_sems, pair_sems, ring_sems, ring_sems, part_sems, part_sems,
-            dma((4,)), dma((4,)), dma((4,)), dma, dma((4,)), dma((3,)), dma, dma,
-            dma, dma, dma, dma((4,)),
+            dma((4,)), dma((4,)), dma((4,)), dma((4,)), dma((4,)), dma((3,)), dma, dma,
+            dma, dma, dma((4,)), dma((4,)),
         ],
         compiler_params=pltpu.CompilerParams(
             collective_id=0, has_side_effects=True, vmem_limit_bytes=56 * 1024 * 1024

time: 119 us -> 114 us (0.958)
  Pallas kernels: 118 us -> 113 us
    pallas_call x1, Pallas kernels: 118 us -> 113 us  [experts(): pl.pallas_call(expert_kernel, out_shape=jax.ShapeDtypeStruct((group, colu...]
where the time goes in v4:
time: 114 us
  Pallas kernels  113 us (99%)
  local copies, waits for them, and re-layouts  1.47 us (1%)
    pallas_call x1, Pallas kernels, experts(): pl.pallas_call(expert_kernel, out_shape=jax.ShapeDtypeStruct((group, colu...  113 us

profile of v4, /device:TPU:1, one launch (start us, length us, event | category | flops | bytes accessed | tf_op | source)
XLA Modules:
  0.0 114.2 jit_solution(3993832105735470272)
XLA Ops:
  0.0 112.7 %shard_map.91 = bf16[64,512]{1,0:T(8,128)(2,1)} custom-call(bf16[64,512]{1,0:T(8,128)(2,1)} %tokens_ref.1, s32[8,64]{1,0:T(8,128)} %bitcast.14, f32[8,64]{1,0:T(8,128)} %bitcast.15, s32[32]{0:T(128)} %placement_ref.1, s32[32]{0:T(128)} %split_ref.1, bf16[8192,128]{1,0:T(8,128)(2,1)} %bitcast.10, bf16[128,4096]{1,0:T(8,128)(2,1)} %bitcast.11, ...), custom_call_target="tpu_custom_call" | custom-call | tf_op jit(solution)/shard_map/pallas_call | solution.py:543
  112.7 1.5 %copy.11 = bf16[64,512]{1,0:T(8,128)(2,1)} copy(bf16[64,512]{1,0:T(8,128)(2,1)} %shard_map.91) | data formatting | bytes 131072

commit v5 on v4

--- a/solution.py
+++ b/solution.py
@@ -16,7 +16,7 @@
 
 
 def parts(chunk):
-    return 1 if chunk < 2 else 2
+    return 1 if chunk < 1 else 2
 CW, CCW = 0, 1
 
 
@@ -460,7 +460,7 @@
         events.append((chunk + 9, 4, -chunk, "finish", chunk, 0))
     events.append((0, 9, 0, "prepare", 0, 0))
     events.append((0, 0, 9, "peers", 0, 0))
-    events.append((1, 0, -0.5, "extra", 0, 0))
+    events.append((0, 0, 10, "extra", 0, 0))
     for _, _, _, kind, chunk, hop in sorted(events):
         if kind == "feat":
             arrive(chunk, hop) if hop else begin(chunk)

time: 114 us -> 113 us (level)
  no operation moved by 1% of the time
where the time goes in v5:
time: 113 us
  Pallas kernels  112 us (99%)
  local copies, waits for them, and re-layouts  1.47 us (1%)
    pallas_call x1, Pallas kernels, experts(): pl.pallas_call(expert_kernel, out_shape=jax.ShapeDtypeStruct((group, colu...  112 us

profile of v5, /device:TPU:1, one launch (start us, length us, event | category | flops | bytes accessed | tf_op | source)
XLA Modules:
  0.0 113.2 jit_solution(17687691289496516008)
XLA Ops:
  0.0 111.7 %shard_map.91 = bf16[64,512]{1,0:T(8,128)(2,1)} custom-call(bf16[64,512]{1,0:T(8,128)(2,1)} %tokens_ref.1, s32[8,64]{1,0:T(8,128)} %bitcast.14, f32[8,64]{1,0:T(8,128)} %bitcast.15, s32[32]{0:T(128)} %placement_ref.1, s32[32]{0:T(128)} %split_ref.1, bf16[8192,128]{1,0:T(8,128)(2,1)} %bitcast.10, bf16[128,4096]{1,0:T(8,128)(2,1)} %bitcast.11, ...), custom_call_target="tpu_custom_call" | custom-call | tf_op jit(solution)/shard_map/pallas_call | solution.py:543
  111.7 1.5 %copy.11 = bf16[64,512]{1,0:T(8,128)(2,1)} copy(bf16[64,512]{1,0:T(8,128)(2,1)} %shard_map.91) | data formatting | bytes 131072

commit v6 on v5

--- a/solution.py
+++ b/solution.py
@@ -483,22 +483,28 @@
     pltpu.make_async_copy(landed, landed, back_recv).wait()
     own_back.wait()
 
-    def weigh(i, table):
-        return jnp.dot(combine[2 * i], table, preferred_element_type=F32) + jnp.dot(
-            combine[2 * i + 1], table, preferred_element_type=F32
-        )
-
-    mix[...] = weigh(0, back[:, :columns])
+    def weigh(i, who, table):
+        return jnp.dot(combine[2 * i, who, :], table, preferred_element_type=F32) + jnp.dot(
+            combine[2 * i + 1, who, :], table, preferred_element_type=F32
+        )
+
     side = pl.ds(pl.multiple_of(core * out_half, out_half), out_half)
-    mix[:, side] += weigh(1, back[:, columns:])
+
+    def mix_group(which):
+        who = pl.ds(pl.multiple_of(which * group, group), group)
+        mix[who, :] = weigh(0, who, back[:, :columns])
+        mix[who, side] += weigh(1, who, back[:, columns:])
+
+    mix_group(1 - core)
     mix_swap = pltpu.make_async_remote_copy(
         src_ref=mix.at[pl.ds((1 - core) * group, group)], dst_ref=mix_sibling,
         send_sem=swap_send.at[2], recv_sem=swap_recv.at[2],
         device_id=sibling, device_id_type=MESH,
     )
     mix_swap.start()
+    mix_group(core)
     mix_swap.wait_recv()
-    out_ref[...] = (mix[pl.ds(pl.multiple_of(core * group, group), group), :] + mix_sibling[...]).astype(BF16)
+    out_ref[...] = (mix[pl.ds(pl.multiple_of(core * group, group), group), :] + mix_sibling[...]).astype(out_ref.dtype)
 
     mix_swap.wait_send()
     extra_swap.wait_send()
@@ -542,7 +548,7 @@
     in_hbm = pl.BlockSpec(memory_space=pl.ANY)
     return pl.pallas_call(
         expert_kernel,
-        out_shape=jax.ShapeDtypeStruct((group, columns), BF16),
+        out_shape=jax.ShapeDtypeStruct((group, columns), F32),
         in_specs=[in_vmem] * 3 + [in_smem] * 2 + [in_hbm] * 4,
         out_specs=in_vmem,
         scratch_shapes=[
@@ -592,7 +598,7 @@
     ws = jnp.transpose(spare_gate_up[0], (1, 2, 0)).reshape(-1, spare_gate_up.shape[1])
     return experts(
         tokens, expert_ids.T, gate_logits.T, placement, split_rows, wh, ws, down_weight[0], spare_down[0]
-    )
+    ).astype(BF16)
 
 
 def solution(mesh):

time: 113 us -> 113 us (level)
  other arithmetic: 0 us -> 1.54 us
  local copies, waits for them, and re-layouts: 1.47 us -> 0 us
    convert_element_type x0 -> x1, other arithmetic: none -> 1.54 us  [per_device(): return experts(tokens, expert_ids.T, gate_logits.T, placement, split_rows...]
    unnamed x1 -> x0, local copies, waits for them, and re-layouts: 1.47 us -> none
where the time goes in v6:
time: 113 us
  Pallas kernels  112 us (99%)
  other arithmetic  1.54 us (1%)
    pallas_call x1, Pallas kernels, experts(): pl.pallas_call(expert_kernel, out_shape=jax.ShapeDtypeStruct((group, colu...  112 us

profile of v6, /device:TPU:1, one launch (start us, length us, event | category | flops | bytes accessed | tf_op | source)
XLA Modules:
  0.0 113.3 jit_solution(4755100235919592096)
XLA Ops:
  0.0 111.8 %shard_map.91 = f32[64,512]{1,0:T(8,128)} custom-call(bf16[64,512]{1,0:T(8,128)(2,1)} %tokens_ref.1, s32[8,64]{1,0:T(8,128)} %bitcast.14, f32[8,64]{1,0:T(8,128)} %bitcast.15, s32[32]{0:T(128)} %placement_ref.1, s32[32]{0:T(128)} %split_ref.1, bf16[8192,128]{1,0:T(8,128)(2,1)} %bitcast.10, bf16[128,4096]{1,0:T(8,128)(2,1)} %bitcast.11, ...), custom_call_target="tpu_custom_call" | custom-call | tf_op jit(solution)/shard_map/pallas_call | solution.py:549
  111.8 1.5 %convert_element_type.3 = bf16[64,512]{1,0:T(8,128)(2,1)} convert(f32[64,512]{1,0:T(8,128)} %shard_map.91) | non-fusion elementwise | flops 32768 | bytes 196608 | tf_op jit(solution)/shard_map/convert_element_type | solution.py:601
